TPU v7x, 512 devices: a whole 4x8x8 slice. The times are simulated.
512 devices in a mesh: gz: 16 (over z, core), xy: 32 (over x, y).
Axes of the slice: x: 4, y: 8, z: 8, core: 2. Of those that a mesh axis runs over, the one named last changes fastest.
Arguments:
- tile_image: bfloat16 [16, 32, 4, 4, 2, 128], P('gz', 'xy'), may hold values from -6 to 6
- tile_target: bfloat16 [16, 32, 4, 3, 4, 2, 128], P('gz', 'xy'), may hold values from 0 to 1
- owner_counts: int32 [16, 32], P('gz', 'xy'), may hold values from 0 to 4, as said below
- tile_list: int32 [16, 32, 4], P('gz', 'xy'), may hold values from -1 to 63, as said below
- w_in: bfloat16 [27, 32], replicated, may hold values from -1.25 to 1.25
- w_res: bfloat16 [27, 32, 32], replicated, may hold values from -0.21875 to 0.21875
- w_down: bfloat16 [8, 64, 32], replicated, may hold values from -0.375 to 0.375
- w_mid: bfloat16 [27, 64, 64], replicated, may hold values from -0.15625 to 0.15625
- w_up: bfloat16 [8, 32, 64], replicated, may hold values from -0.75 to 0.75
- head_weight: bfloat16 [3, 32], replicated, may hold values from -1 to 1
Outputs:
- err_tiles: bfloat16 [16, 32, 4, 3, 4, 2, 128], P('gz', 'xy')
- grad_in: float32 [27, 32], replicated
- grad_res: float32 [27, 32, 32], replicated
- grad_down: float32 [8, 64, 32], replicated
- grad_mid: float32 [27, 64, 64], replicated
- grad_up: float32 [8, 32, 64], replicated
- head_weight_gradient: float32 [3, 32], replicated
Inputs may be any that keep to these rules, and one draw needn't show every extreme that they name: `owner_counts`: in each depth row the counts add up to 64, and some owner of every row holds exactly 4 tiles. `tile_list`: in each depth row the live slots (s < owner_counts) name every position 0 to 63 exactly once; the other slots hold -1.
All inputs are finite; a program needn't handle non-finite values.
Results may differ from a plain program's by a relative error of at most 0.0046.
Values may be sent and summed in bfloat16 or wider, within the bound.
A program may use at most 64 MiB of HBM per device.

v0:
```python
import jax
import jax.numpy as jnp
from jax import lax
from jax.sharding import PartitionSpec as P

TPD = 2


def with_halo(cells, sides, width):
    for axis, dim in sides:
        count = lax.axis_size(axis)
        ends = count - 1
        head = lax.slice_in_dim(cells, 0, width, axis=dim)
        tail = lax.slice_in_dim(cells, cells.shape[dim] - width, cells.shape[dim], axis=dim)
        cells = jnp.concatenate(
            [
                lax.ppermute(tail, axis, [(i, (i + 1) % count) for i in range(ends)]),
                cells,
                lax.ppermute(head, axis, [((i + 1) % count, i) for i in range(ends)]),
            ],
            axis=dim,
        )
    return cells


def framed(field):
    padded = with_halo(field, (("gz", 1), ("xy", 3)), 1)
    return jnp.pad(padded, ((0, 0), (0, 0), (1, 1), (0, 0)))


def convolve(padded, weights):
    depth = padded.shape[1] - 2
    height = padded.shape[2] - 2
    width = padded.shape[3] - 2
    total = None
    for tap in range(27):
        off_z, off_y, off_x = (tap // 9, tap // 3 % 3, tap % 3)
        window = padded[:, off_z : off_z + depth, off_y : off_y + height, off_x : off_x + width]
        term = jnp.einsum("oc,czyx->ozyx", weights[tap], window, preferred_element_type=jnp.float32)
        total = term if total is None else total + term
    return total


def tap_grads(grad, padded):
    depth, height, width = grad.shape[1:]
    terms = []
    for tap in range(27):
        off_z, off_y, off_x = (tap // 9, tap // 3 % 3, tap % 3)
        window = padded[:, off_z : off_z + depth, off_y : off_y + height, off_x : off_x + width]
        terms.append(jnp.einsum("ozyx,czyx->oc", grad, window, preferred_element_type=jnp.float32))
    return jnp.stack(terms)


def flipped(weights):
    return jnp.transpose(weights[::-1], (0, 2, 1))


def strided(field, tap):
    return field[:, tap // 4 :: 2, tap // 2 % 2 :: 2, tap % 2 :: 2]


def alternate(parts):
    chans, depth, height, width = parts.shape[1:]
    return (
        parts.reshape(2, 2, 2, chans, depth, height, width)
        .transpose(3, 4, 0, 5, 1, 6, 2)
        .reshape(chans, 2 * depth, 2 * height, 2 * width)
    )


def local(
    tile_image, tile_target, owner_counts, tile_list, w_in, w_res, w_down, w_mid, w_up, head_weight
):
    single_float = jnp.float32
    brain_float_half = jnp.bfloat16
    ranks = lax.axis_size("xy")
    layers = lax.axis_size("gz")
    column = lax.axis_index("xy")
    slots = tile_list.shape[2]
    depth, height, width = (tile_image.shape[3], tile_image.shape[4], tile_image.shape[5])
    per_dev = TPD
    total_tiles = ranks * per_dev
    slot_list = tile_list[0, 0]
    live = jnp.arange(slots) < owner_counts[0, 0]
    select = ((slot_list[None, :] == jnp.arange(total_tiles)[:, None]) & live[None, :]).astype(
        brain_float_half
    )
    wanted = column * per_dev + jnp.arange(per_dev)
    piece_img = lax.all_gather(tile_image, "xy", axis=1, tiled=True)
    piece_tgt = lax.all_gather(tile_target, "xy", axis=1, tiled=True)
    piece_cnt = lax.all_gather(owner_counts, "xy", axis=1, tiled=True)
    piece_list = lax.all_gather(tile_list, "xy", axis=1, tiled=True)
    owners = piece_list.shape[1]
    piece_live = jnp.arange(slots)[None, :] < piece_cnt[0][:, None]
    match = ((piece_list[0][:, :, None] == wanted[None, None, :]) & piece_live[:, :, None]).astype(
        brain_float_half
    )
    acc_img = jnp.einsum(
        "kst,kszyx->tzyx", match, piece_img[0], preferred_element_type=single_float
    )
    acc_tgt = jnp.einsum(
        "kst,ksazyx->tazyx", match, piece_tgt[0], preferred_element_type=single_float
    )
    rows_hit = (jnp.arange(ranks)[:, None] == jnp.arange(owners)[None, :]).astype(single_float)
    acc_hit = jnp.dot(rows_hit, jnp.sum(match.astype(single_float), axis=1))
    acc_img, acc_tgt, acc_hit = (acc_img, acc_tgt, acc_hit)
    mine_img = acc_img.astype(brain_float_half)
    mine_tgt = acc_tgt.astype(brain_float_half)
    owner_hit = acc_hit.astype(brain_float_half)
    image = mine_img.transpose(1, 2, 0, 3).reshape(1, depth, height, per_dev * width)
    target = mine_tgt.transpose(1, 2, 3, 0, 4).reshape(3, depth, height, per_dev * width)
    voxel_cells = depth * height * per_dev * width * ranks * layers
    image_pad = framed(image)
    h0 = jax.nn.relu(convolve(image_pad, w_in[:, :, None])).astype(brain_float_half)
    h0_pad = framed(h0)
    h1 = jax.nn.relu(h0.astype(single_float) + convolve(h0_pad, w_res)).astype(brain_float_half)
    down_sum = None
    for tap in range(8):
        term = jnp.einsum(
            "oc,czyx->ozyx", w_down[tap], strided(h1, tap), preferred_element_type=single_float
        )
        down_sum = term if down_sum is None else down_sum + term
    dfield = jax.nn.relu(down_sum).astype(brain_float_half)
    dfield_pad = framed(dfield)
    cfield = jax.nn.relu(dfield.astype(single_float) + convolve(dfield_pad, w_mid)).astype(
        brain_float_half
    )
    upward = alternate(
        jnp.stack(
            [
                jnp.einsum("oc,czyx->ozyx", w_up[tap], cfield, preferred_element_type=single_float)
                for tap in range(8)
            ]
        )
    )
    signal_field = jax.nn.relu(h1.astype(single_float) + upward).astype(brain_float_half)
    logits = jnp.einsum(
        "ac,czyx->azyx", head_weight, signal_field, preferred_element_type=single_float
    )
    affinity_map = jax.nn.sigmoid(logits)
    error_field = affinity_map - target.astype(single_float)
    err_out = error_field.astype(brain_float_half)
    err_local = err_out.reshape(3, depth, height, per_dev, width).transpose(3, 0, 1, 2, 4)
    sending = owner_hit[:, :, None, None, None, None] * err_local[None]
    returned = lax.all_to_all(sending, "xy", split_axis=0, concat_axis=0, tiled=True)
    returned = returned.reshape((total_tiles, 3, depth, height, width))
    err_tiles = jnp.einsum(
        "ps,pazyx->sazyx", select, returned, preferred_element_type=single_float
    ).astype(brain_float_half)[None, None]
    logit_gradient = (error_field * affinity_map * (1.0 - affinity_map) / voxel_cells).astype(
        brain_float_half
    )
    head_weight_gradient = jnp.einsum(
        "mtnq,btnq->mb", logit_gradient, signal_field, preferred_element_type=single_float
    )
    gradient_total = jnp.einsum(
        "jn,jbrq->nbrq", head_weight, logit_gradient, preferred_element_type=single_float
    )
    gsf = jnp.where(signal_field > 0, gradient_total, 0.0).astype(brain_float_half)
    grad_up = jnp.stack(
        [
            jnp.einsum(
                "ozyx,czyx->oc", strided(gsf, tap), cfield, preferred_element_type=single_float
            )
            for tap in range(8)
        ]
    )
    gcoarse = None
    for tap in range(8):
        term = jnp.einsum(
            "oc,ozyx->czyx", w_up[tap], strided(gsf, tap), preferred_element_type=single_float
        )
        gcoarse = term if gcoarse is None else gcoarse + term
    gquad = jnp.where(cfield > 0, gcoarse, 0.0).astype(brain_float_half)
    grad_mid = tap_grads(gquad, dfield_pad)
    gdown = gquad.astype(single_float) + convolve(framed(gquad), flipped(w_mid))
    gdd = jnp.where(dfield > 0, gdown, 0.0).astype(brain_float_half)
    grad_down = jnp.stack(
        [
            jnp.einsum("ozyx,czyx->oc", gdd, strided(h1, tap), preferred_element_type=single_float)
            for tap in range(8)
        ]
    )
    spread = alternate(
        jnp.stack(
            [
                jnp.einsum("oc,ozyx->czyx", w_down[tap], gdd, preferred_element_type=single_float)
                for tap in range(8)
            ]
        )
    )
    gres = jnp.where(h1 > 0, gsf.astype(single_float) + spread, 0.0).astype(brain_float_half)
    grad_res = tap_grads(gres, h0_pad)
    gfirst = gres.astype(single_float) + convolve(framed(gres), flipped(w_res))
    gact = jnp.where(h0 > 0, gfirst, 0.0).astype(brain_float_half)
    grad_in = tap_grads(gact, image_pad)[:, :, 0]
    summed = lax.psum(
        (grad_in, grad_res, grad_down, grad_mid, grad_up, head_weight_gradient), ("gz", "xy")
    )
    return (err_tiles, summed[0], summed[1], summed[2], summed[3], summed[4], summed[5])


def solution(mesh):
    return jax.shard_map(
        local,
        mesh=mesh,
        in_specs=(
            P("gz", "xy", None, None, None, None),
            P("gz", "xy", None, None, None, None, None),
            P("gz", "xy"),
            P("gz", "xy", None),
            P(),
            P(),
            P(),
            P(),
            P(),
            P(),
        ),
        out_specs=(P("gz", "xy", None, None, None, None, None), P(), P(), P(), P(), P(), P()),
        check_vma=False,
    )
```

profile of v0, /device:TPU:1, one launch (start us, length us, event | category | flops | bytes accessed | tf_op | source)
XLA Modules:
  0.0 600.4 jit_solution(4131910350337606113)
XLA Ops:
  7.9 1.3 dynamic-slice
  9.8 18.0 %all-reduce.3 = s32[32]{0:T(128)S(1)} all-reduce(s32[32]{0:T(128)S(1)} %bitcast_dynamic-update-slice_fusion), channel_id=1, replica_groups=mesh['gz'=16,'xy'=32] {'xy'}, use_global_device_ids=true, to_apply=%add.3 | all-reduce | flops 32 | bytes 256
  27.9 25.2 %all_gather.12 = s32[1,32,4]{2,0,1:T(1,128)S(1)} all-gather(s32[1,1,4]{2,0,1:T(1,128)} %bitcast.2102), channel_id=1, replica_groups=mesh['gz'=16,'xy'=32] {'xy'}, dimensions={1}, use_global_device_ids=true | all-gather | bytes 528 | tf_op jit(solution)/shard_map/all_gather | solution.py:92
  53.9 35.7 %all_gather.14 = bf16[1,32,4,4,2,128]{5,3,4,2,0,1:T(4,128)(2,1)S(1)} all-gather(bf16[1,1,4,4,2,128]{5,3,4,2,0,1:T(4,128)(2,1)S(1)} %copy.229), channel_id=1, replica_groups=mesh['gz'=16,'xy'=32] {'xy'}, dimensions={1}, use_global_device_ids=true | all-gather | bytes 270336 | tf_op jit(solution)/shard_map/all_gather | solution.py:89
  89.8 29.0 %collective-permute-start = (bf16[1,1,2,256]{3,2,1,0:T(2,128)(2,1)S(1)}, bf16[1,1,2,256]{3,2,1,0:T(2,128)(2,1)S(1)}, u32[]{:S(2)}, u32[]{:S(2)}) collective-permute-start(bf16[1,1,2,256]{3,2,1,0:T(2,128)(2,1)S(1)} %get-tuple-element.194), channel_id=1, source_target_pairs={{0,32},{32,64},{64,96},{96,128},{128,160},{160,192},{192,224},{224... | collective-permute-start | bytes 3080 | tf_op jit(solution)/shard_map/ppermute | solution.py:17
  118.8 1.9 collective-permute-start.1
  120.7 1.0 bitcast_convert_fusion.52
  121.7 0.9 bitcast_convert_fusion.51
  122.7 0.8 fusion.359
  123.5 0.8 fusion.350
  124.3 0.8 fusion.340
  126.2 36.3 %all_gather.15 = bf16[1,32,4,3,4,2,128]{6,4,5,3,2,0,1:T(4,128)(2,1)S(1)} all-gather(bf16[1,1,4,3,4,2,128]{6,4,5,3,2,0,1:T(4,128)(2,1)S(1)} %copy.234), channel_id=1, replica_groups=mesh['gz'=16,'xy'=32] {'xy'}, dimensions={1}, use_global_device_ids=true | all-gather | bytes 811008 | tf_op jit(solution)/shard_map/all_gather | solution.py:90
  167.3 1.9 collective-permute-start.2
  169.2 1.3 collective-permute-start.3
  170.5 3.0 collective-permute-done.3
  173.7 0.8 slice_bitcast_fusion.108
  175.9 17.0 %collective-permute-start.4 = (bf16[32,1,2,256]{3,0,2,1:T(8,128)(2,1)S(1)}, bf16[32,1,2,256]{3,0,2,1:T(8,128)(2,1)S(1)}, u32[]{:S(2)}, u32[]{:S(2)}) collective-permute-start(bf16[32,1,2,256]{3,0,2,1:T(8,128)(2,1)S(1)} %get-tuple-element.91), channel_id=1, source_target_pairs={{0,32},{32,64},{64,96},{96,128},{128,160},{160,192},{192,224},{224... | collective-permute-start | bytes 98312 | tf_op jit(solution)/shard_map/ppermute | solution.py:17
  192.9 1.9 collective-permute-start.5
  195.0 3.1 collective-permute-done.5
  198.2 2.3 collective-permute-start.6
  200.6 1.3 collective-permute-start.7
  202.2 3.7 collective-permute-done.7
  217.7 1.9 fusion.751
  219.6 1.0 fusion.752
  222.4 3.3 collective-permute-start.8
  225.7 1.9 collective-permute-start.9
  227.8 3.0 collective-permute-done.9
  230.9 4.1 collective-permute-start.10
  234.9 1.5 collective-permute-start.11
  236.5 3.7 collective-permute-done.11
  256.1 3.1 collective-permute-start.12
  259.2 1.9 collective-permute-start.13
  261.2 1.1 broadcast_multiply_fusion
  262.3 9.4 %all-to-all-start = ((bf16[32,2,3,4,2,128]{5,1,4,3,2,0:T(2,128)(2,1)}), bf16[32,2,3,4,2,128]{5,1,4,3,2,0:T(2,128)(2,1)S(1)}, u32[]{:S(2)}, u32[]{:S(2)}) async-start(bf16[32,2,3,4,2,128]{5,1,4,3,2,0:T(2,128)(2,1)} %broadcast_multiply_fusion), calls=%async_computation | async-start | bytes 786432 | tf_op jit(solution)/shard_map/all_to_all | solution.py:145
  271.9 1.3 collective-permute-start.15
  273.2 4.0 collective-permute-start.14
  277.3 6.3 %collective-permute-done.15 = bf16[64,4,1,1]{3,0,1,2:T(8,128)(2,1)S(1)} collective-permute-done((bf16[64,4,1,1]{3,0,1,2:T(8,128)(2,1)S(1)}, bf16[64,4,1,1]{3,0,1,2:T(8,128)(2,1)S(1)}, u32[]{:S(2)}, u32[]{:S(2)}) %collective-permute-start.15) | collective-permute-done | bytes 544 | tf_op jit(solution)/shard_map/ppermute | solution.py:19
  294.1 3.3 collective-permute-start.16
  297.4 1.9 collective-permute-start.17
  301.0 1.7 collective-permute-done.17
  302.8 2.6 collective-permute-start.18
  305.5 1.5 collective-permute-start.19
  307.2 3.7 collective-permute-done.19
  321.0 111.3 %all-reduce.4 = (f32[27,32]{1,0:T(8,128)}, f32[3,32]{1,0:T(4,128)}) all-reduce(f32[27,32]{1,0:T(8,128)S(1)} %bitcast.2093, f32[3,32]{1,0:T(4,128)S(1)} %convolution_bitcast_fusion.112), channel_id=1, replica_groups=mesh['gz'=16,'xy'=32] {'gz','xy'}, use_global_device_ids=true, to_apply=%region_1.2 | all-reduce | flops 960 | bytes 7680 | tf_op jit(solution)/shard_map/psum | solution.py:197
  433.6 154.9 %all-reduce.8.cloned.1.call-done = (f32[27,32,32]{2,1,0:T(8,128)}, f32[8,64,32]{1,2,0:T(8,128)}, f32[27,64,64]{2,1,0:T(8,128)}, f32[8,32,64]{2,1,0:T(8,128)}) async-done(((f32[27,32,32]{2,1,0:T(8,128)}, f32[8,64,32]{1,2,0:T(8,128)}, f32[27,64,64]{2,1,0:T(8,128)}, f32[8,32,64]{2,1,0:T(8,128)}), (f32[27,32,32]{2,1,0:T(8,128)}, f32[8,64,32]{1,2,0:T(8,128)}, f32[27,64,64]{2,1,0:T(8,128)}, ...) | async-done | bytes 684048 | tf_op jit(solution)/shard_map/psum | solution.py:197
  588.5 1.9 copy.810
  590.4 1.6 copy.811
  592.0 0.9 copy.812
  (498 shorter events, 62.8 us)
Async XLA Ops:
  7.2 237.8 %copy-start = (bf16[3,32]{1,0:T(4,128)(2,1)S(1)}, bf16[3,32]{1,0:T(4,128)(2,1)}, u32[]{:S(2)}) copy-start(bf16[3,32]{1,0:T(4,128)(2,1)} %param.19) | copy-start | bytes 580
  7.2 118.0 %copy-start.1 = (bf16[27,64,64]{2,1,0:T(8,128)(2,1)S(1)}, bf16[27,64,64]{2,1,0:T(8,128)(2,1)}, u32[]{:S(2)}) copy-start(bf16[27,64,64]{2,1,0:T(8,128)(2,1)} %param.17) | copy-start | bytes 663556
  89.8 76.7 %collective-permute-start = (bf16[1,1,2,256]{3,2,1,0:T(2,128)(2,1)S(1)}, bf16[1,1,2,256]{3,2,1,0:T(2,128)(2,1)S(1)}, u32[]{:S(2)}, u32[]{:S(2)}) collective-permute-start(bf16[1,1,2,256]{3,2,1,0:T(2,128)(2,1)S(1)} %get-tuple-element.194), channel_id=1, source_target_pairs={{0,32},{32,64},{64,96},{96,128},{128,160},{160,192},{192,224},{224... | collective-permute-start | bytes 3080 | tf_op jit(solution)/shard_map/ppermute | solution.py:17
  118.8 47.8 %collective-permute-start.1 = (bf16[1,1,2,256]{3,2,1,0:T(2,128)(2,1)S(1)}, bf16[1,1,2,256]{3,2,1,0:T(2,128)(2,1)S(1)}, u32[]{:S(2)}, u32[]{:S(2)}) collective-permute-start(bf16[1,1,2,256]{3,2,1,0:T(2,128)(2,1)S(1)} %get-tuple-element.193), channel_id=1, source_target_pairs={{32,0},{64,32},{96,64},{128,96},{160,128},{192,160},{224,192},{256... | collective-permute-start | bytes 3080 | tf_op jit(solution)/shard_map/ppermute | solution.py:19
  126.1 37.7 %copy-start.4 = (bf16[27,32,32]{2,1,0:T(8,128)(2,1)S(1)}, bf16[27,32,32]{2,1,0:T(8,128)(2,1)}, u32[]{:S(2)}) copy-start(bf16[27,32,32]{2,1,0:T(8,128)(2,1)} %param.15) | copy-start | bytes 165892
  167.3 3.3 collective-permute-start.2
  169.2 4.3 collective-permute-start.3
  175.9 19.1 %collective-permute-start.4 = (bf16[32,1,2,256]{3,0,2,1:T(8,128)(2,1)S(1)}, bf16[32,1,2,256]{3,0,2,1:T(8,128)(2,1)S(1)}, u32[]{:S(2)}, u32[]{:S(2)}) collective-permute-start(bf16[32,1,2,256]{3,0,2,1:T(8,128)(2,1)S(1)} %get-tuple-element.91), channel_id=1, source_target_pairs={{0,32},{32,64},{64,96},{96,128},{128,160},{160,192},{192,224},{224... | collective-permute-start | bytes 98312 | tf_op jit(solution)/shard_map/ppermute | solution.py:17
  192.9 5.2 collective-permute-start.5
  198.2 4.0 collective-permute-start.6
  200.6 5.4 collective-permute-start.7
  212.4 8.2 %copy-start.25 = (bf16[32,2,1,128]{3,0,2,1:T(8,128)(2,1)}, bf16[32,2,1,128]{3,0,2,1:T(8,128)(2,1)S(1)}, u32[]{:S(2)}) copy-start(bf16[32,2,1,128]{3,0,2,1:T(8,128)(2,1)S(1)} %slice.1254) | copy-start | bytes 49156
  213.2 7.6 %copy-start.23 = (bf16[32,2,1,128]{3,0,2,1:T(8,128)(2,1)}, bf16[32,2,1,128]{3,0,2,1:T(8,128)(2,1)S(1)}, u32[]{:S(2)}) copy-start(bf16[32,2,1,128]{3,0,2,1:T(8,128)(2,1)S(1)} %slice.1256) | copy-start | bytes 49156
  214.0 7.1 %copy-start.21 = (bf16[32,2,1,128]{3,0,2,1:T(8,128)(2,1)}, bf16[32,2,1,128]{3,0,2,1:T(8,128)(2,1)S(1)}, u32[]{:S(2)}) copy-start(bf16[32,2,1,128]{3,0,2,1:T(8,128)(2,1)S(1)} %slice.1258) | copy-start | bytes 49156
  214.7 6.6 %copy-start.19 = (bf16[32,2,1,128]{3,0,2,1:T(8,128)(2,1)}, bf16[32,2,1,128]{3,0,2,1:T(8,128)(2,1)S(1)}, u32[]{:S(2)}) copy-start(bf16[32,2,1,128]{3,0,2,1:T(8,128)(2,1)S(1)} %slice.1260) | copy-start | bytes 49156
  215.5 6.0 %copy-start.17 = (bf16[32,2,1,128]{3,0,2,1:T(8,128)(2,1)}, bf16[32,2,1,128]{3,0,2,1:T(8,128)(2,1)S(1)}, u32[]{:S(2)}) copy-start(bf16[32,2,1,128]{3,0,2,1:T(8,128)(2,1)S(1)} %slice.1262) | copy-start | bytes 49156
  216.2 5.5 copy-start.15
  217.0 4.9 copy-start.13
  217.7 4.4 copy-start.11
  222.4 5.4 collective-permute-start.8
  225.7 5.1 collective-permute-start.9
  230.9 9.6 %collective-permute-start.10 = (bf16[64,4,1,1]{3,0,1,2:T(8,128)(2,1)S(1)}, bf16[64,4,1,1]{3,0,1,2:T(8,128)(2,1)S(1)}, u32[]{:S(2)}, u32[]{:S(2)}) collective-permute-start(bf16[64,4,1,1]{3,0,1,2:T(8,128)(2,1)S(1)} %get-tuple-element.95), channel_id=1, source_target_pairs={{0,1},{1,2},{2,3},{3,4},{4,5},{5,6},{6,7},{7,8},{8,9},{9,10},{10,1... | collective-permute-start | bytes 1544 | tf_op jit(solution)/shard_map/ppermute | solution.py:17
  234.9 5.3 collective-permute-start.11
  254.6 7.7 %copy-start.9 = (f32[8,32,64]{2,1,0:T(8,128)}, f32[8,32,64]{2,1,0:T(8,128)S(1)}, u32[]{:S(2)}) copy-start(f32[8,32,64]{2,1,0:T(8,128)S(1)} %fusion.113) | copy-start | bytes 196612
  254.6 6.6 %copy-start.53 = (bf16[32,2]{1,0:T(8,128)(2,1)S(1)}, bf16[32,2]{1,0:T(8,128)(2,1)}, u32[]{:S(2)}) copy-start(bf16[32,2]{1,0:T(8,128)(2,1)} %copy.228) | copy-start | bytes 388
  256.1 27.7 %copy-start.8 = (f32[2,128,64]{1,2,0:T(8,128)S(1)}, f32[2,128,64]{1,2,0:T(8,128)}, u32[]{:S(2)}) copy-start(f32[2,128,64]{1,2,0:T(8,128)} %convolution_add_fusion.31) | copy-start | bytes 196612
  256.1 15.6 %collective-permute-start.12 = (bf16[64,1,1,128]{3,0,1,2:T(8,128)(2,1)S(1)}, bf16[64,1,1,128]{3,0,1,2:T(8,128)(2,1)S(1)}, u32[]{:S(2)}, u32[]{:S(2)}) collective-permute-start(bf16[64,1,1,128]{3,0,1,2:T(8,128)(2,1)S(1)} %get-tuple-element.99), channel_id=1, source_target_pairs={{0,32},{32,64},{64,96},{96,128},{128,160},{160,192},{192,224},{224... | collective-permute-start | bytes 49160 | tf_op jit(solution)/shard_map/ppermute | solution.py:17
  259.2 12.6 %collective-permute-start.13 = (bf16[64,1,1,128]{3,0,1,2:T(8,128)(2,1)S(1)}, bf16[64,1,1,128]{3,0,1,2:T(8,128)(2,1)S(1)}, u32[]{:S(2)}, u32[]{:S(2)}) collective-permute-start(bf16[64,1,1,128]{3,0,1,2:T(8,128)(2,1)S(1)} %get-tuple-element.100), channel_id=1, source_target_pairs={{32,0},{64,32},{96,64},{128,96},{160,128},{192,160},{224,192},{256... | collective-permute-start | bytes 49160 | tf_op jit(solution)/shard_map/ppermute | solution.py:19
  262.3 21.9 %copy-start.2 = (f32[27,64,64]{2,1,0:T(8,128)}, f32[27,64,64]{2,1,0:T(8,128)S(1)}, u32[]{:S(2)}) copy-start(f32[27,64,64]{2,1,0:T(8,128)S(1)} %constant_dynamic-update-slice_fusion.3) | copy-start | bytes 1327108
  262.3 170.0 %all-to-all-start = ((bf16[32,2,3,4,2,128]{5,1,4,3,2,0:T(2,128)(2,1)}), bf16[32,2,3,4,2,128]{5,1,4,3,2,0:T(2,128)(2,1)S(1)}, u32[]{:S(2)}, u32[]{:S(2)}) async-start(bf16[32,2,3,4,2,128]{5,1,4,3,2,0:T(2,128)(2,1)} %broadcast_multiply_fusion), calls=%async_computation | async-start | bytes 786432 | tf_op jit(solution)/shard_map/all_to_all | solution.py:145
  271.7 316.8 %all-reduce.8.cloned.1.call-start = ((), (), s32[]{:S(2)}) async-start(), calls=%async_computation.1 | async-start | bytes 3178496 | tf_op jit(solution)/shard_map/psum | solution.py:197
  271.9 11.7 %collective-permute-start.15 = (bf16[64,4,1,1]{3,0,1,2:T(8,128)(2,1)S(1)}, bf16[64,4,1,1]{3,0,1,2:T(8,128)(2,1)S(1)}, u32[]{:S(2)}, u32[]{:S(2)}) collective-permute-start(bf16[64,4,1,1]{3,0,1,2:T(8,128)(2,1)S(1)} %get-tuple-element.94), channel_id=1, source_target_pairs={{1,0},{2,1},{3,2},{4,3},{5,4},{6,5},{7,6},{8,7},{9,8},{10,9},{11,1... | collective-permute-start | bytes 1544 | tf_op jit(solution)/shard_map/ppermute | solution.py:19
  273.2 10.6 %collective-permute-start.14 = (bf16[64,4,1,1]{3,0,1,2:T(8,128)(2,1)S(1)}, bf16[64,4,1,1]{3,0,1,2:T(8,128)(2,1)S(1)}, u32[]{:S(2)}, u32[]{:S(2)}) collective-permute-start(bf16[64,4,1,1]{3,0,1,2:T(8,128)(2,1)S(1)} %get-tuple-element.93), channel_id=1, source_target_pairs={{0,1},{1,2},{2,3},{3,4},{4,5},{5,6},{6,7},{7,8},{8,9},{9,10},{10,1... | collective-permute-start | bytes 1544 | tf_op jit(solution)/shard_map/ppermute | solution.py:17
  285.3 2.1 copy-start.16
  285.3 2.2 copy-start.14
  293.2 6.3 %copy-start.30 = (bf16[32,4,2,256]{3,0,2,1:T(8,128)(2,1)S(1)}, bf16[32,4,2,256]{3,0,2,1:T(8,128)(2,1)}, u32[]{:S(2)}) copy-start(bf16[32,4,2,256]{3,0,2,1:T(8,128)(2,1)} %get-tuple-element.67) | copy-start | bytes 393220
  293.4 6.3 %copy-start.29 = (bf16[32,4,2,256]{3,0,2,1:T(8,128)(2,1)S(1)}, bf16[32,4,2,256]{3,0,2,1:T(8,128)(2,1)}, u32[]{:S(2)}) copy-start(bf16[32,4,2,256]{3,0,2,1:T(8,128)(2,1)} %get-tuple-element.51) | copy-start | bytes 393220
  293.5 6.2 %copy-start.28 = (bf16[32,4,2,256]{3,0,2,1:T(8,128)(2,1)S(1)}, bf16[32,4,2,256]{3,0,2,1:T(8,128)(2,1)}, u32[]{:S(2)}) copy-start(bf16[32,4,2,256]{3,0,2,1:T(8,128)(2,1)} %get-tuple-element.50) | copy-start | bytes 393220
  293.7 6.2 %copy-start.27 = (bf16[32,4,2,256]{3,0,2,1:T(8,128)(2,1)S(1)}, bf16[32,4,2,256]{3,0,2,1:T(8,128)(2,1)}, u32[]{:S(2)}) copy-start(bf16[32,4,2,256]{3,0,2,1:T(8,128)(2,1)} %get-tuple-element.49) | copy-start | bytes 393220
  293.9 6.2 %copy-start.12 = (bf16[32,2,1,128]{3,0,2,1:T(8,128)(2,1)S(1)}, bf16[32,2,1,128]{3,0,2,1:T(8,128)(2,1)}, u32[]{:S(2)}) copy-start(bf16[32,2,1,128]{3,0,2,1:T(8,128)(2,1)} %copy-done.11) | copy-start | bytes 49156
  294.1 6.9 %collective-permute-start.16 = (bf16[32,1,2,256]{3,0,2,1:T(8,128)(2,1)S(1)}, bf16[32,1,2,256]{3,0,2,1:T(8,128)(2,1)S(1)}, u32[]{:S(2)}, u32[]{:S(2)}) collective-permute-start(bf16[32,1,2,256]{3,0,2,1:T(8,128)(2,1)S(1)} %get-tuple-element.81), channel_id=1, source_target_pairs={{0,32},{32,64},{64,96},{96,128},{128,160},{160,192},{192,224},{224... | collective-permute-start | bytes 98312 | tf_op jit(solution)/shard_map/ppermute | solution.py:17
  297.4 5.3 collective-permute-start.17
  302.8 4.3 collective-permute-start.18
  305.5 5.4 collective-permute-start.19
  320.0 112.6 %copy-start.81 = (s32[1,1,4]{2,1,0:T(1,128)S(1)}, s32[1,1,4]{2,1,0:T(1,128)}, u32[]{:S(2)}) copy-start(s32[1,1,4]{2,1,0:T(1,128)} %param.13) | copy-start | bytes 52
  320.0 112.7 %copy-start.82 = (pred[4]{0:T(512)(128)(4,1)S(1)}, pred[4]{0:T(512)(128)(4,1)}, u32[]{:S(2)}) copy-start(pred[4]{0:T(512)(128)(4,1)} %iota_compare_fusion.8) | copy-start | bytes 16
  588.5 3.5 copy-start.3
  590.4 2.5 copy-start.51
  (57 other events, 74.1 us)
Sparse Core Ops, SparseCore 0:
  301.1 287.3 all-reduce.7
where the time goes:
time: 603 us; the launch traced here: 600 us
  blocking collectives  226 us (37%)
  waiting for transfers between devices  183 us (30%)
  starting transfers between devices  96.5 us (16%)
  matrix products  39.2 us (7%)
  local copies, waits for them, and re-layouts  30.5 us (5%)
  between operations  16.6 us (3%)
  other arithmetic  7.79 us (1%)
    psum x1, waiting for transfers between devices, local(): lax.psum((grad_in, grad_res, grad_down, grad_mid, grad_up, head_weight_gr...  155 us
    psum x1, blocking collectives, local(): lax.psum((grad_in, grad_res, grad_down, grad_mid, grad_up, head_weight_gr...  111 us
    ppermute x10, starting transfers between devices, with_halo(): lax.ppermute(tail, axis, [(i, (i + 1) % count) for i in range(ends)])  70.6 us
    all_gather x1, blocking collectives, local(): piece_tgt = lax.all_gather(tile_target, 'xy', axis=1, tiled=True)  36.3 us
    all_gather x1, blocking collectives, local(): piece_img = lax.all_gather(tile_image, 'xy', axis=1, tiled=True)  35.7 us
    ppermute x10, waiting for transfers between devices, with_halo(): lax.ppermute(head, axis, [((i + 1) % count, i) for i in range(ends)])  28.3 us
    all_gather x1, blocking collectives, local(): piece_list = lax.all_gather(tile_list, 'xy', axis=1, tiled=True)  25.2 us
    dot_general x108, matrix products, convolve(): jnp.einsum('oc,czyx->ozyx', weights[tap], window, preferred_element_type=...  20.8 us
  transfers between devices with their start and end apart: 22, of which 10 were waited for; matrix products, arithmetic and copies ran while one was open for 6% of the time, Pallas kernels for 0%

commit v1 on v0

v1 whole, which is shorter than its diff:
```python
import functools

import jax
import jax.numpy as jnp
from jax import lax
from jax.experimental import pallas as pl
from jax.experimental.pallas import tpu as pltpu
from jax.sharding import PartitionSpec as P

F32 = jnp.float32
BF16 = jnp.bfloat16
MESH = pl.DeviceIdType.MESH
SLOTS = 4
CORES = 2
ROWS = 1024
VM = pl.BlockSpec(memory_space=pltpu.VMEM)

RES, MID, DOWN, UP, INP, HEAD, USED = 0, 288, 672, 800, 928, 992, 1000


def grid_of(ranks):
    height = 8 if ranks == 32 else 2
    return ranks // height, height


def remote(src, dst, send, recv, where):
    return pltpu.make_async_remote_copy(
        src_ref=src, dst_ref=dst, send_sem=send, recv_sem=recv, device_id=where, device_id_type=MESH
    )


def greet(peers):
    barrier = pltpu.get_barrier_semaphore()
    for peer in peers:
        pl.semaphore_signal(barrier, inc=1, device_id=peer, device_id_type=MESH)
    pl.semaphore_wait(barrier, len(peers))


def spread_kernel(
    nx, ny, ng, block, halo, full, meta, xg, placed, yr, mine, hr, xs, xr, ys, yw, hs, hw
):
    ranks = nx * ny
    g = lax.axis_index("gz")
    j = lax.axis_index("xy")
    xi = j // ny
    yi = lax.rem(j, ny)
    x_peer = [(g, lax.rem(xi + k, nx) * ny + yi) for k in range(nx)]
    y_peer = [(g, xi * ny + lax.rem(yi + k, ny)) for k in range(ny)]
    around = [(dz, dj) for dz in (0, -1, 1, -2, 2) for dj in (0, -1, 1) if (dz, dj) != (0, 0)]
    near = [(lax.rem(g + dz + ng, ng), lax.rem(j + dj + ranks, ranks)) for dz, dj in around]
    greet(x_peer[1:] + y_peer[1:] + near)

    steps = [remote(block, xg.at[k], xs.at[k], xr.at[k], x_peer[k]) for k in range(1, nx)]
    for copy in steps:
        copy.start()
    xg[0] = block[...]
    for copy in steps:
        copy.wait()
    for k in range(nx):
        meta[k] = xg[k, 128:144, :]

    def place(k):
        first = ((xi * ny + lax.rem(yi + k, ny)) * 2).astype(F32)
        sums = [jnp.zeros((32, 128), F32), jnp.zeros((32, 128), F32)]
        for a in range(nx):
            names = xg[a, 128:144, :].astype(F32)
            for s in range(SLOTS):
                tile = xg[a, s * 32 : (s + 1) * 32, :].astype(F32)
                name = names[s : s + 1]
                for t in range(2):
                    sums[t] = sums[t] + jnp.where(name == first + t, tile, 0.0)
        for t in range(2):
            placed[k, t] = sums[t].astype(BF16)

    def y_copy(k):
        return remote(
            placed.at[k],
            yr.at[k],
            ys.at[k],
            yw.at[k],
            (g, xi * ny + lax.rem(yi + k, ny)),
        )

    def send_one(k, carry):
        place(k)
        y_copy(k).start()
        return carry

    lax.fori_loop(1, ny, send_one, 0)
    place(0)
    total = placed[0].astype(F32)
    for k in range(1, ny):
        y_copy(k).wait()
        total = total + yr[k].astype(F32)
    mine[...] = total.astype(BF16)

    copies = []
    for n, (dz, dj) in enumerate(around):
        rows = slice(0, 16) if abs(dz) == 2 else slice(0, 32)
        if dj == 0:
            src, dst = mine.at[:, rows], hr.at[2 - dz, 1:3, rows]
        elif dj == 1:
            src, dst = mine.at[1, rows], hr.at[2 - dz, 0, rows]
        else:
            src, dst = mine.at[0, rows], hr.at[2 - dz, 3, rows]
        copies.append(remote(src, dst, hs.at[n], hw.at[n], near[n]))
    for copy in copies:
        copy.start()
    hr[2, 1:3] = mine[...]
    for copy in copies:
        copy.wait()
    for z in range(5):
        halo[z] = hr[z, :, 0:16]
    for z in range(3):
        full[z] = hr[z + 1]


def spread_tiles(nx, ny, ng, block):
    return pl.pallas_call(
        functools.partial(spread_kernel, nx, ny, ng),
        out_shape=(
            jax.ShapeDtypeStruct((5, 4, 16, 128), BF16),
            jax.ShapeDtypeStruct((3, 4, 32, 128), BF16),
            jax.ShapeDtypeStruct((nx, 16, 128), BF16),
        ),
        in_specs=[VM],
        out_specs=(VM, VM, VM),
        scratch_shapes=[
            pltpu.VMEM((nx, 144, 128), BF16),
            pltpu.VMEM((ny, 2, 32, 128), BF16),
            pltpu.VMEM((ny, 2, 32, 128), BF16),
            pltpu.VMEM((2, 32, 128), BF16),
            pltpu.VMEM((5, 4, 32, 128), BF16),
            pltpu.SemaphoreType.DMA((nx,)),
            pltpu.SemaphoreType.DMA((nx,)),
            pltpu.SemaphoreType.DMA((ny,)),
            pltpu.SemaphoreType.DMA((ny,)),
            pltpu.SemaphoreType.DMA((14,)),
            pltpu.SemaphoreType.DMA((14,)),
        ],
        compiler_params=pltpu.CompilerParams(
            collective_id=0, has_side_effects=True, vmem_limit_bytes=32 << 20
        ),
        name="spread",
    )(block)


def iota(shape, dim):
    return lax.broadcasted_iota(jnp.int32, shape, dim)


def dot(a, b):
    return jnp.dot(a, b, preferred_element_type=F32)


def dot_t(a, b):
    return lax.dot_general(a, b, (((1,), (1,)), ((), ())), preferred_element_type=F32)


def hot(cond):
    return jnp.where(cond, 1.0, 0.0).astype(BF16)


def eye(n):
    return hot(iota((n, n), 0) == iota((n, n), 1))


def before(v):
    return pltpu.roll(v, 1, 1)


def after(v):
    return pltpu.roll(v, v.shape[1] - 1, 1)


def put_fine(buf, at, v):
    prev = before(v[128:256]).astype(BF16)
    succ = after(v[0:128]).astype(BF16)
    even = v[0:128].astype(BF16)
    odd = v[128:256].astype(BF16)
    for zo in range(2):
        for yo in range(2):
            rows = slice(zo * 64 + yo * 32, zo * 64 + yo * 32 + 32)
            for n, part in enumerate((prev, even, odd, succ)):
                buf[at + zo, yo * 128 + n * 32 : yo * 128 + n * 32 + 32, :] = part[rows]


def put_coarse(buf, at, v):
    buf[at, 0:64, :] = before(v).astype(BF16)
    buf[at, 64:128, :] = v.astype(BF16)
    buf[at, 128:192, :] = after(v).astype(BF16)
    buf[at, 192:256, :] = jnp.zeros((64, v.shape[1]), BF16)


def tap_of(pos):
    return (pos >> 1 & 1) * 4 + (pos & 1) * 2 + (pos >> 2)


def step_kernel(
    nz,
    nx_cells,
    voxels,
    halo,
    full,
    w_in,
    w_res,
    w_down,
    w_mid,
    w_up,
    head,
    vec,
    err_ref,
    w0,
    w1,
    w1b,
    wm,
    wmb,
    tcol,
    tgt,
    h0s,
    c0,
    h1s,
    cd,
    qs,
    ss,
    gls,
    gss,
    cg,
    gds,
    cr,
    grs,
    gas,
    errs,
):
    g = lax.axis_index("gz")
    j = lax.axis_index("xy")
    wide = 256

    i32, i64 = eye(32), eye(64)
    for xo in range(2):
        fwd = jnp.zeros((288, 128), F32)
        for c in range(3):
            put = hot(iota((32, 128), 1) == iota((32, 128), 0) + 32 * (c + xo))
            fwd = fwd + dot(w_res[:, c].reshape(288, 32), put)
        fwd = fwd.astype(BF16)
        blank = jnp.zeros((32, 32), BF16)
        for zy in range(9):
            parts = [w_res[8 - zy, 2 - c] for c in range(3)]
            parts = [blank] + parts if xo else parts + [blank]
            bwd = dot_t(i32, jnp.concatenate(parts, axis=0)).astype(BF16)
            dz, dy = zy // 3, zy % 3
            for zo in range(2):
                for yo in range(2):
                    y_in = yo + dy - 1
                    if 0 <= y_in < 2:
                        rows = slice(xo * 128 + zo * 64 + yo * 32, xo * 128 + zo * 64 + yo * 32 + 32)
                        lanes = slice((zo + dz) * 256 + y_in * 128, (zo + dz) * 256 + y_in * 128 + 128)
                        w1[rows, lanes] = fwd[zy * 32 : zy * 32 + 32]
                        w1b[rows, lanes] = bwd
        for zo in range(2):
            for yo in range(2):
                rows = slice(xo * 128 + zo * 64 + yo * 32, xo * 128 + zo * 64 + yo * 32 + 32)
                lanes = slice((3 - 3 * zo) * 256, (3 - 3 * zo) * 256 + 256)
                w1[rows, lanes] = jnp.zeros((32, 256), BF16)
                w1b[rows, lanes] = jnp.zeros((32, 256), BF16)
    taps_t = dot_t(i32, w_in[...]).astype(BF16)
    col = iota((27, 32), 1)
    tap = iota((27, 32), 0)
    for pos in range(8):
        xo, zo, yo = pos >> 2, pos >> 1 & 1, pos & 1
        hit = jnp.zeros((27, 32), jnp.bool_)
        for t in range(27):
            dz, dy, dx = t // 9, t // 3 % 3, t % 3
            if 0 <= yo + dy - 1 < 2:
                at = (zo + dz) * 8 + (xo + dx) * 2 + yo + dy - 1
                hit = hit | ((tap == t) & (col == at))
        w0[pos * 32 : pos * 32 + 32, :] = dot(taps_t, hot(hit)).astype(BF16)
    wd_t = jnp.concatenate([dot_t(i32, w_down[tap_of(p)]) for p in range(8)], axis=0).astype(BF16)
    wd = dot_t(i64, wd_t).astype(BF16)
    wu = jnp.concatenate([w_up[tap_of(p)] for p in range(8)], axis=0)
    wu_t = dot_t(i64, wu).astype(BF16)
    blank = jnp.zeros((64, 64), BF16)
    for a in range(3):
        fwd = [dot_t(i64, w_mid[9 * a + 3 + c]).astype(BF16) for c in range(3)] + [blank]
        bwd = [w_mid[26 - (9 * a + 3 + c)] for c in range(3)] + [blank]
        wm[:, a * 256 : a * 256 + 256] = dot_t(i64, jnp.concatenate(fwd, axis=0)).astype(BF16)
        wmb[:, a * 256 : a * 256 + 256] = dot_t(i64, jnp.concatenate(bwd, axis=0)).astype(BF16)
    heads = dot(head[...], hot((iota((32, 256), 1) & 31) == iota((32, 256), 0)))
    hd = jnp.concatenate(
        [jnp.broadcast_to(heads[a : a + 1], (8, 256)) for a in range(3)]
        + [jnp.zeros((8, 256), F32)],
        axis=0,
    )
    same = (iota((32, 256), 0) & 7) == (iota((32, 256), 1) >> 5)
    hd = jnp.where(same, hd, 0.0).astype(BF16)
    hd_t = dot_t(eye(256), hd).astype(BF16)

    image = jnp.concatenate(
        [
            jnp.concatenate([halo[z, t].astype(F32)[0:8] for t in range(4)], axis=1)
            for z in range(5)
        ],
        axis=0,
    )
    z2 = iota((40, 512), 0) + 8 * g - 16
    x1 = iota((40, 512), 1) + 256 * j - 128
    inside = (z2 >= 0) & (z2 < 4 * nz) & (x1 >= 0) & (x1 < 2 * nx_cells)
    image = jnp.where(inside, image, 0.0).astype(BF16)
    place = iota((512, wide), 0)
    lane2 = 2 * iota((512, wide), 1) + 128
    pick = [hot(place == ((lane2 + k) & 511)) for k in (-1, 0, 1, 2)]
    parts = jnp.concatenate([dot(image, p) for p in pick], axis=0).astype(BF16)
    r = iota((176, 160), 0)
    zi = r >> 3
    source = ((r >> 1) & 3) * 40 + (zi - 1) * 2 + (r & 1)
    order = hot((iota((176, 160), 1) == source) & (zi >= 1) & (zi <= 20))
    tcol[...] = dot(order, parts).astype(BF16)
    target = jnp.concatenate(
        [
            jnp.concatenate([full[z, t].astype(F32)[8:32] for t in range(4)], axis=1)
            for z in range(3)
        ],
        axis=0,
    ).astype(BF16)
    parts = jnp.concatenate([dot(target, p) for p in pick[1:3]], axis=0).astype(BF16)
    r = iota((192, 144), 0)
    source = (
        ((r >> 2) & 1) * 72
        + (r >> 6) * 24
        + ((r >> 3) & 3) * 8
        + (((r >> 5) & 1) * 2 + ((r >> 1) & 1)) * 2
        + (r & 1)
    )
    order = hot((iota((192, 144), 1) == source) & (((r >> 3) & 3) < 3))
    placed = dot(order, parts)
    for n in range(6):
        tgt[n] = placed[n * 32 : n * 32 + 32]

    lane = iota((1, wide), 1)
    cell = jnp.where(lane < 192, lane, lane - 256) + 128 * j
    lane_in = jnp.where((cell >= 0) & (cell < nx_cells), 1.0, 0.0)

    def in_slab(zc):
        at = 2 * g + zc
        return lane_in * jnp.where((at >= 0) & (at < nz), 1.0, 0.0)

    def first_conv(n, carry):
        rows = tcol[pl.ds(pl.multiple_of(n * 16, 16), 32), :]
        h0 = jnp.maximum(dot(w0[...], rows), 0.0) * in_slab(n - 4)
        h0s[n] = h0.astype(BF16)
        put_fine(c0, 2 * n, h0)
        return carry

    lax.fori_loop(0, 10, first_conv, 0)

    def second_conv(n, carry):
        cols = c0[pl.ds(2 * n + 1, 4)].reshape(1024, wide)
        h1 = jnp.maximum(h0s[n + 1].astype(F32) + dot(w1[...], cols), 0.0).astype(BF16)
        h1s[n] = h1
        put_coarse(cd, n, jnp.maximum(dot(wd, h1), 0.0) * in_slab(n - 3))
        return carry

    lax.fori_loop(0, 8, second_conv, 0)

    def middle(n, carry):
        cols = cd[pl.ds(n, 3)].reshape(768, wide)
        q = jnp.maximum(cd[n + 1, 64:128].astype(F32) + dot(wm[...], cols), 0.0).astype(BF16)
        qs[n] = q
        s = jnp.maximum(h1s[n + 1].astype(F32) + dot(wu, q), 0.0).astype(BF16)
        ss[n] = s
        aff = jax.nn.sigmoid(dot(hd, s))
        err = aff - tgt[n]
        errs[n] = err.astype(BF16)
        gl = (err * aff * (1.0 - aff) / voxels).astype(BF16)
        gls[n] = gl
        gs = jnp.where(s.astype(F32) > 0, dot(hd_t, gl), 0.0).astype(BF16)
        gss[n] = gs
        gq = jnp.where(q.astype(F32) > 0, dot(wu_t, gs), 0.0) * in_slab(n - 2)
        put_coarse(cg, n, gq)
        return carry

    lax.fori_loop(0, 6, middle, 0)

    def back(n, carry):
        cols = cg[pl.ds(n, 3)].reshape(768, wide)
        gdd = cg[n + 1, 64:128].astype(F32) + dot(wmb[...], cols)
        gdd = jnp.where(cd[n + 2, 64:128].astype(F32) > 0, gdd, 0.0).astype(BF16)
        gds[n] = gdd
        gr = gss[n + 1].astype(F32) + dot(wd_t, gdd)
        gr = jnp.where(h1s[n + 2].astype(F32) > 0, gr, 0.0) * in_slab(n - 1)
        grs[n] = gr.astype(BF16)
        put_fine(cr, 2 * n, gr)
        return carry

    lax.fori_loop(0, 4, back, 0)

    for n in range(2):
        cols = cr[2 * n + 1 : 2 * n + 5, :, 0:128].reshape(1024, 128)
        ga = grs[n + 1, :, 0:128].astype(F32) + dot(w1b[...], cols)
        gas[n] = jnp.where(h0s[n + 4, :, 0:128].astype(F32) > 0, ga, 0.0).astype(BF16)

    def own(ref, first):
        return jnp.concatenate([ref[first, :, 0:128], ref[first + 1, :, 0:128]], axis=1)

    rows = jnp.concatenate([errs[2, :, 0:128], errs[3, :, 0:128]], axis=0)
    src = iota((128, 256), 0)
    dst = iota((128, 256), 1)
    parts = jnp.concatenate([dot(rows, hot(dst == 2 * src + xo)) for xo in range(2)], axis=0)
    r = iota((32, 128), 0)
    source = ((r >> 2) & 1) * 32 + (r >> 3) * 8 + ((r >> 1) & 1) * 2 + (r & 1)
    q = iota((32, 128), 1)
    order = hot((q == source) | (q == source + 68))
    tiles = dot(order, parts.astype(BF16))
    err_ref[...] = jnp.concatenate([tiles[0:24, 0:128], tiles[0:24, 128:256]], axis=0).astype(BF16)

    gr = own(grs, 1)
    for zi in range(4):
        for yi in range(2):
            lanes = slice(yi * 128, yi * 128 + 128)
            cols = jnp.concatenate([c0[7 + zi, lanes, 0:128], c0[9 + zi, lanes, 0:128]], axis=1)
            part = dot_t(gr, cols)
            for zo in range(2):
                for yo in range(2):
                    dz, dy = zi - zo, yi - yo + 1
                    if 0 <= dz < 3:
                        rows = zo * 64 + yo * 32
                        both = part[rows : rows + 32] + pltpu.roll(
                            part[128 + rows : 128 + rows + 32], 96, 1
                        )
                        at = RES + (dz * 3 + dy) * 32
                        if zi == dz and yi == max(dy - 1, 0):
                            vec[at : at + 32, :] = both
                        else:
                            vec[at : at + 32, :] += both
    gq = jnp.concatenate([cg[2, 64:128, 0:128], cg[3, 64:128, 0:128]], axis=1)
    for a in range(3):
        for half in range(2):
            lanes = slice(half * 128, half * 128 + 128)
            cols = jnp.concatenate([cd[2 + a, lanes, 0:128], cd[3 + a, lanes, 0:128]], axis=1)
            at = MID + (a * 2 + half) * 64
            vec[at : at + 64, :] = dot_t(gq, cols)
    gdd = own(gds, 1)
    down = dot_t(gdd, own(h1s, 3))
    vec[DOWN : DOWN + 64, :] = down[:, 0:128]
    vec[DOWN + 64 : DOWN + 128, :] = down[:, 128:256]
    gs = own(gss, 2)
    qq = own(qs, 2)
    none = jnp.zeros((64, 256), BF16)
    vec[UP : UP + 128, :] = dot_t(gs[0:128], jnp.concatenate([qq, none], axis=0)) + dot_t(
        gs[128:256], jnp.concatenate([none, qq], axis=0)
    )
    cols = jnp.concatenate([tcol[64:96, 0:128], tcol[80:112, 0:128]], axis=1)
    inp = dot_t(cols, own(gas, 0))
    vec[INP : INP + 32, :] = inp[:, 0:128]
    vec[INP + 32 : INP + 64, :] = inp[:, 128:256]
    heads = jnp.where(same, dot_t(own(gls, 2), own(ss, 2)), 0.0)
    vec[HEAD:ROWS, :] = jnp.zeros((ROWS - HEAD, 128), F32)
    for a in range(3):
        line = jnp.sum(heads[a * 8 : a * 8 + 8], axis=0, keepdims=True)
        line = line[:, 0:128] + line[:, 128:256]
        line = line + pltpu.roll(line, 64, 1)
        line = line + pltpu.roll(line, 32, 1)
        vec[HEAD + a : HEAD + a + 1, :] = line


def local_step(nz, nx_cells, voxels, halo, full, w_in, w_res, w_down, w_mid, w_up, head):
    wide = 256
    return pl.pallas_call(
        functools.partial(step_kernel, nz, nx_cells, float(voxels)),
        out_shape=(
            jax.ShapeDtypeStruct((ROWS, 128), F32),
            jax.ShapeDtypeStruct((48, 128), BF16),
        ),
        in_specs=[VM] * 8,
        out_specs=(VM, VM),
        scratch_shapes=[
            pltpu.VMEM((256, 32), BF16),
            pltpu.VMEM((256, 1024), BF16),
            pltpu.VMEM((256, 1024), BF16),
            pltpu.VMEM((64, 768), BF16),
            pltpu.VMEM((64, 768), BF16),
            pltpu.VMEM((176, wide), BF16),
            pltpu.VMEM((6, 32, wide), F32),
            pltpu.VMEM((10, 256, wide), BF16),
            pltpu.VMEM((20, 256, wide), BF16),
            pltpu.VMEM((8, 256, wide), BF16),
            pltpu.VMEM((8, 256, wide), BF16),
            pltpu.VMEM((6, 64, wide), BF16),
            pltpu.VMEM((6, 256, wide), BF16),
            pltpu.VMEM((6, 32, wide), BF16),
            pltpu.VMEM((6, 256, wide), BF16),
            pltpu.VMEM((6, 256, wide), BF16),
            pltpu.VMEM((4, 64, wide), BF16),
            pltpu.VMEM((8, 256, wide), BF16),
            pltpu.VMEM((4, 256, wide), BF16),
            pltpu.VMEM((2, 256, 128), BF16),
            pltpu.VMEM((6, 32, wide), BF16),
        ],
        compiler_params=pltpu.CompilerParams(vmem_limit_bytes=48 << 20),
        name="step",
    )(halo, full, w_in, w_res, w_down, w_mid, w_up, head)


def sum_kernel(
    nx,
    ny,
    nzc,
    vec,
    err,
    meta,
    out,
    tiles,
    rc,
    ac,
    rx,
    ax,
    ry,
    ay,
    rz,
    gy,
    gx,
    gc,
    ey,
    em,
    ex,
    cs,
    cw,
    xs,
    xw,
    ys,
    yw,
    zs,
    zw,
    eys,
    eyw,
    exs,
    exw,
    gys,
    gyw,
    gxs,
    gxw,
):
    g = lax.axis_index("gz")
    j = lax.axis_index("xy")
    xi = j // ny
    yi = lax.rem(j, ny)
    zi = g // CORES
    core = lax.rem(g, CORES)
    other = (zi * CORES + 1 - core, j)
    x_at = [lax.rem(xi + k, nx) for k in range(nx)]
    y_at = [lax.rem(yi + k, ny) for k in range(ny)]
    x_peer = [(g, x_at[k] * ny + yi) for k in range(nx)]
    y_peer = [(g, xi * ny + y_at[k]) for k in range(ny)]
    z_peer = [(lax.rem(zi + k, nzc) * CORES + core, j) for k in range(nzc)]
    greet([other] + x_peer[1:] + y_peer[1:] + z_peer[1:])

    swap = remote(vec.at[1 - core], rc, cs.at[0], cw.at[0], other)
    swap.start()
    to_y = [remote(err, ey.at[k], eys.at[k], eyw.at[k], y_peer[k]) for k in range(1, ny)]
    for copy in to_y:
        copy.start()
    ey[0] = err[...]
    swap.wait_recv()
    ac[...] = vec[core] + rc[...]
    over_x = [remote(ac.at[x_at[k]], rx.at[k], xs.at[k], xw.at[k], x_peer[k]) for k in range(1, nx)]
    for copy in over_x:
        copy.start()

    for copy in to_y:
        copy.wait_recv()
    def answer(a, carry):
        names = meta[a].astype(F32)
        sums = [jnp.zeros((24, 128), F32) for _ in range(SLOTS)]
        for k in range(ny):
            first = ((xi * ny + lax.rem(yi - k + ny, ny)) * 2).astype(F32)
            pair = ey[k].astype(F32)
            for t in range(2):
                for s in range(SLOTS):
                    sums[s] = sums[s] + jnp.where(
                        names[s : s + 1] == first + t, pair[t * 24 : t * 24 + 24], 0.0
                    )
        em[a] = jnp.concatenate(sums, axis=0).astype(BF16)
        return carry

    lax.fori_loop(0, nx, answer, 0)
    to_x = [
        remote(em.at[nx - k], ex.at[k], exs.at[k], exw.at[k], x_peer[k]) for k in range(1, nx)
    ]
    for copy in to_x:
        copy.start()

    for copy in over_x:
        copy.wait_recv()
    total = ac[xi]
    for k in range(1, nx):
        total = total + rx[k]
    ax[...] = total
    over_y = [remote(ax.at[y_at[k]], ry.at[k], ys.at[k], yw.at[k], y_peer[k]) for k in range(1, ny)]
    for copy in over_y:
        copy.start()
    for copy in over_y:
        copy.wait_recv()
    total = ax[yi]
    for k in range(1, ny):
        total = total + ry[k]
    ay[...] = total
    over_z = [remote(ay, rz.at[zi], zs.at[k], zw.at[k], z_peer[k]) for k in range(1, nzc)]
    for copy in over_z:
        copy.start()
    rz[zi] = ay[...]
    for k in range(1, nzc):
        remote(ay, rz.at[lax.rem(zi - k + nzc, nzc)], zs.at[k], zw.at[k], z_peer[k]).wait_recv()
    total = rz[0]
    for k in range(1, nzc):
        total = total + rz[k]
    gy[yi] = total
    back_y = [remote(gy.at[yi], gy.at[yi], gys.at[k], gyw.at[k], y_peer[k]) for k in range(1, ny)]
    for copy in back_y:
        copy.start()
    for k in range(1, ny):
        at = lax.rem(yi - k + ny, ny)
        remote(gy.at[at], gy.at[at], gys.at[k], gyw.at[k], y_peer[k]).wait_recv()
    gx[xi] = gy[...]
    back_x = [remote(gx.at[xi], gx.at[xi], gxs.at[k], gxw.at[k], x_peer[k]) for k in range(1, nx)]
    for copy in back_x:
        copy.start()
    for k in range(1, nx):
        at = lax.rem(xi - k + nx, nx)
        remote(gx.at[at], gx.at[at], gxs.at[k], gxw.at[k], x_peer[k]).wait_recv()
    back = remote(gx, gc, cs.at[1], cw.at[1], other)
    back.start()
    out[core] = gx[...]

    for copy in to_x:
        copy.wait_recv()
    total = em[0].astype(F32)
    for k in range(1, nx):
        total = total + ex[k].astype(F32)
    tiles[...] = total.astype(BF16)

    back.wait_recv()
    out[1 - core] = gc[...]
    for copy in [swap, back] + to_y + over_x + to_x + over_y + over_z + back_y + back_x:
        copy.wait_send()


def sum_all(nx, ny, nzc, vec, err, meta):
    rows = ROWS // (CORES * nx * ny)
    pair = [pltpu.SemaphoreType.DMA((2,))] * 2
    on_x = [pltpu.SemaphoreType.DMA((nx,))] * 2
    on_y = [pltpu.SemaphoreType.DMA((ny,))] * 2
    on_z = [pltpu.SemaphoreType.DMA((nzc,))] * 2
    return pl.pallas_call(
        functools.partial(sum_kernel, nx, ny, nzc),
        out_shape=(
            jax.ShapeDtypeStruct((CORES, nx, ny, rows, 128), F32),
            jax.ShapeDtypeStruct((96, 128), BF16),
        ),
        in_specs=[VM] * 3,
        out_specs=(VM, VM),
        scratch_shapes=[
            pltpu.VMEM((nx, ny, rows, 128), F32),
            pltpu.VMEM((nx, ny, rows, 128), F32),
            pltpu.VMEM((nx, ny, rows, 128), F32),
            pltpu.VMEM((ny, rows, 128), F32),
            pltpu.VMEM((ny, rows, 128), F32),
            pltpu.VMEM((rows, 128), F32),
            pltpu.VMEM((nzc, rows, 128), F32),
            pltpu.VMEM((ny, rows, 128), F32),
            pltpu.VMEM((nx, ny, rows, 128), F32),
            pltpu.VMEM((nx, ny, rows, 128), F32),
            pltpu.VMEM((ny, 48, 128), BF16),
            pltpu.VMEM((nx, 96, 128), BF16),
            pltpu.VMEM((nx, 96, 128), BF16),
        ]
        + pair
        + on_x
        + on_y
        + on_z
        + on_y
        + on_x
        + on_y
        + on_x,
        compiler_params=pltpu.CompilerParams(
            collective_id=1, has_side_effects=True, vmem_limit_bytes=32 << 20
        ),
        name="sums",
    )(vec.reshape(CORES, nx, ny, rows, 128), err, meta)


def unpack_kernel(vec, g_in, g_res, g_down, g_mid, g_up, g_head, lines):
    for zy in range(9):
        strip = vec[RES + zy * 32 : RES + zy * 32 + 32, :]
        for c in range(3):
            part = strip if c == 0 else pltpu.roll(strip, 128 - 32 * c, 1)
            g_res[zy * 3 + c] = part[:, 0:32]
    for t in range(27):
        a, b, c = t // 9, t // 3 % 3, t % 3
        if b == 1:
            at = MID + (a * 2 + c // 2) * 64
            part = vec[at : at + 64, :]
            if c % 2:
                part = pltpu.roll(part, 64, 1)
            g_mid[t] = part[:, 0:64]
        else:
            g_mid[t] = jnp.zeros((64, 64), F32)
    for pos in range(8):
        quarter = pos & 3
        at = DOWN + (pos >> 2) * 64
        part = vec[at : at + 64, :]
        if quarter:
            part = pltpu.roll(part, 128 - 32 * quarter, 1)
        g_down[tap_of(pos)] = part[:, 0:32]
        part = vec[UP + quarter * 32 : UP + quarter * 32 + 32, :]
        if pos >> 2:
            part = pltpu.roll(part, 64, 1)
        g_up[tap_of(pos)] = part[:, 0:64]
        part = vec[INP + (pos >> 2) * 32 : INP + (pos >> 2) * 32 + 32, :]
        if quarter:
            part = pltpu.roll(part, 128 - 32 * quarter, 1)
        lines[pos] = part
    for t in range(27):
        dz, dy, dx = t // 9, t // 3 % 3, t % 3
        total = None
        for pos in range(8):
            xo, zo, yo = pos >> 2, pos >> 1 & 1, pos & 1
            if 0 <= yo + dy - 1 < 2:
                at = (zo + dz) * 8 + (xo + dx) * 2 + yo + dy - 1
                line = lines[pos, at : at + 1, :]
                total = line if total is None else total + line
        g_in[t : t + 1, :] = total[:, 0:32]
    g_head[...] = vec[HEAD : HEAD + 8, :][0:3, 0:32]


def unpack(vec):
    return pl.pallas_call(
        unpack_kernel,
        out_shape=(
            jax.ShapeDtypeStruct((27, 32), F32),
            jax.ShapeDtypeStruct((27, 32, 32), F32),
            jax.ShapeDtypeStruct((8, 64, 32), F32),
            jax.ShapeDtypeStruct((27, 64, 64), F32),
            jax.ShapeDtypeStruct((8, 32, 64), F32),
            jax.ShapeDtypeStruct((3, 32), F32),
        ),
        in_specs=[VM],
        out_specs=(VM,) * 6,
        scratch_shapes=[pltpu.VMEM((8, 32, 128), F32)],
        compiler_params=pltpu.CompilerParams(vmem_limit_bytes=32 << 20),
        name="unpack",
    )(vec)


def local(
    tile_image, tile_target, owner_counts, tile_list, w_in, w_res, w_down, w_mid, w_up, head_weight
):
    ranks = lax.axis_size("xy")
    ng = lax.axis_size("gz")
    nx, ny = grid_of(ranks)
    live = jnp.arange(SLOTS) < owner_counts[0, 0]
    names = jnp.where(live, tile_list[0, 0], -1).astype(BF16)
    names = jnp.broadcast_to(jnp.pad(names, (0, 12))[:, None], (16, 128))
    block = jnp.concatenate(
        [
            jnp.concatenate(
                [tile_image.reshape(SLOTS, 8, 128), tile_target.reshape(SLOTS, 24, 128)], axis=1
            ).reshape(SLOTS * 32, 128),
            names,
        ],
        axis=0,
    )
    halo, full, meta = spread_tiles(nx, ny, ng, block)
    vec, err = local_step(
        2 * ng,
        128 * ranks,
        ng * ranks * 2048,
        halo,
        full,
        w_in,
        w_res.reshape(9, 3, 32, 32),
        w_down,
        w_mid,
        w_up,
        head_weight,
    )
    sums, tiles = sum_all(nx, ny, ng // CORES, vec, err, meta)
    grads = unpack(sums.reshape(ROWS, 128))
    return (tiles.reshape(1, 1, SLOTS, 3, 4, 2, 128),) + tuple(grads)


def solution(mesh):
    return jax.shard_map(
        local,
        mesh=mesh,
        in_specs=(
            P("gz", "xy", None, None, None, None),
            P("gz", "xy", None, None, None, None, None),
            P("gz", "xy"),
            P("gz", "xy", None),
            P(),
            P(),
            P(),
            P(),
            P(),
            P(),
        ),
        out_specs=(P("gz", "xy", None, None, None, None, None), P(), P(), P(), P(), P(), P()),
        check_vma=False,
    )
```

time: 603 us -> 88.7 us (0.15)
  blocking collectives: 226 us -> 0 us
  waiting for transfers between devices: 183 us -> 0 us
  starting transfers between devices: 96.5 us -> 0 us
  Pallas kernels: 0 us -> 81.4 us
  matrix products: 39.2 us -> 0 us
  local copies, waits for them, and re-layouts: 30.5 us -> 4.05 us
  between operations: 16.6 us -> 1.41 us
  other arithmetic: 7.79 us -> 1.5 us
    psum x1 -> x0, waiting for transfers between devices: 155 us -> none  [local(): lax.psum((grad_in, grad_res, grad_down, grad_mid, grad_up, head_weight_gr...]
    psum x1 -> x0, blocking collectives: 111 us -> none  [local(): lax.psum((grad_in, grad_res, grad_down, grad_mid, grad_up, head_weight_gr...]
    all_gather x3 -> x0, blocking collectives: 97.2 us -> none  [the longest x1 36.3 us: local(): piece_tgt = lax.all_gather(tile_target, 'xy', axis=1, tiled=True)]
    ppermute x20 -> x0, starting transfers between devices: 87.1 us -> none  [the longest x10 70.6 us: with_halo(): lax.ppermute(tail, axis, [(i, (i + 1) % count) for i in range(ends)])]
    pallas_call x0 -> x4, Pallas kernels: none -> 81.4 us  [the longest x1 32.6 us: sum_all(): pl.pallas_call(functools.partial(sum_kernel, nx, ny, nzc), out_shape=(jax...]
    dot_general x227 -> x0, matrix products: 39.2 us -> none  [the longest x108 20.8 us: convolve(): jnp.einsum('oc,czyx->ozyx', weights[tap], window, preferred_element_type=...]
    ppermute x20 -> x0, waiting for transfers between devices: 28.4 us -> none  [the longest x10 28.3 us: with_halo(): lax.ppermute(head, axis, [((i + 1) % count, i) for i in range(ends)])]
    unnamed x1 -> x0, blocking collectives: 18 us -> none
  transfers between devices with their start and end apart: 22 -> 0, of which waited for: 10 -> 0; matrix products, arithmetic and copies ran while one was open for 6% -> 0% of each run, Pallas kernels for 0% -> 0%
where the time goes in v1:
time: 88.7 us; the launch traced here: 88.3 us
  Pallas kernels  81.4 us (92%)
  local copies, waits for them, and re-layouts  4.05 us (5%)
  other arithmetic  1.5 us (2%)
  between operations  1.41 us (2%)
    pallas_call x1, Pallas kernels, sum_all(): pl.pallas_call(functools.partial(sum_kernel, nx, ny, nzc), out_shape=(jax...  32.6 us
    pallas_call x1, Pallas kernels, spread_tiles(): pl.pallas_call(functools.partial(spread_kernel, nx, ny, ng), out_shape=(j...  29.4 us
    pallas_call x1, Pallas kernels, local_step(): pl.pallas_call(functools.partial(step_kernel, nz, nx_cells, float(voxels)...  18.2 us
    unnamed x13, local copies, waits for them, and re-layouts  4.05 us

profile of v1, /device:TPU:1, one launch (start us, length us, event | category | flops | bytes accessed | tf_op | source)
XLA Modules:
  0.0 88.3 jit_solution(4961523426605851540)
XLA Ops:
  0.6 0.0 copy-start.1
  1.3 0.7 fusion
  2.0 0.7 pad_maximum_fusion.1
  2.7 0.1 pad_maximum_fusion.block
  2.8 0.0 copy-start.2
  2.9 1.0 %copy.17.w_down = bf16[8,64,32]{2,1,0:T(8,128)(2,1)S(1)} copy(bf16[8,64,32]{1,2,0:T(8,128)(2,1)} %param.16) | data formatting | bytes 65536 | tf_op args[6]
  3.8 0.0 copy-start.3
  3.9 29.4 %spread.1 = (bf16[5,4,16,128]{3,2,1,0:T(8,128)(2,1)S(1)}, bf16[3,4,32,128]{3,2,1,0:T(8,128)(2,1)S(1)}, bf16[4,16,128]{2,1,0:T(8,128)(2,1)S(1)}) custom-call(bf16[144,128]{1,0:T(8,128)(2,1)S(1)} %pad_maximum_fusion.block), custom_call_target="tpu_custom_call" | custom-call | tf_op jit(solution)/shard_map/spread/pallas_call | solution.py:119
  33.2 0.0 copy-start.4
  33.2 0.0 copy-done.1
  33.2 0.0 copy-done.2
  33.2 0.0 copy-done.3
  33.3 0.6 copy-done.4
  33.9 0.0 copy-start
  33.9 1.0 %copy-done = bf16[27,64,64]{2,1,0:T(8,128)(2,1)S(1)} copy-done((bf16[27,64,64]{2,1,0:T(8,128)(2,1)S(1)}, bf16[27,64,64]{2,1,0:T(8,128)(2,1)}, u32[]{:S(2)}) %copy-start) | copy-done | bytes 221208
  34.9 18.2 %step.1 = (f32[1024,128]{1,0:T(8,128)S(1)}, bf16[48,128]{1,0:T(8,128)(2,1)S(1)}) custom-call(bf16[5,4,16,128]{3,2,1,0:T(8,128)(2,1)S(1)} %get-tuple-element.20.halo, bf16[3,4,32,128]{3,2,1,0:T(8,128)(2,1)S(1)} %get-tuple-element.21.full, bf16[27,32]{1,0:T(8,128)(2,1)S(1)} %copy-done.3, bf16[9,3,32,32]{3,2,1,0:T(8,128)(2,1)S(1)} %bitcast.13, ...), custom_call_target="tpu_custom_call" | custom-call | tf_op jit(solution)/shard_map/step/pallas_call | solution.py:468
  53.1 32.6 %sums.1 = (f32[2,4,8,16,128]{4,3,2,1,0:T(8,128)S(1)}, bf16[96,128]{1,0:T(8,128)(2,1)S(1)}) custom-call(f32[2,4,8,16,128]{4,3,2,1,0:T(8,128)S(1)} %bitcast.12, bf16[48,128]{1,0:T(8,128)(2,1)S(1)} %get-tuple-element.23.err, bf16[4,16,128]{2,1,0:T(8,128)(2,1)S(1)} %get-tuple-element.24.meta), custom_call_target="tpu_custom_call" | custom-call | tf_op jit(solution)/shard_map/sums/pallas_call | solution.py:653
  85.7 1.2 %unpack.1 = (f32[27,32]{1,0:T(8,128)}, f32[27,32,32]{2,1,0:T(8,128)}, f32[8,64,32]{2,1,0:T(8,128)S(1)}, f32[27,64,64]{2,1,0:T(8,128)}, f32[8,32,64]{2,1,0:T(8,128)}, /*index=5*/f32[3,32]{1,0:T(4,128)}) custom-call(f32[1024,128]{1,0:T(8,128)S(1)} %bitcast.11), custom_call_target="tpu_custom_call" | custom-call | tf_op jit(solution)/shard_map/unpack/pallas_call | solution.py:736
  86.9 0.8 copy.18
  87.7 0.6 copy.21
  (1 shorter events, 0.0 us)
Async XLA Ops:
  0.6 32.6 %copy-start.1 = (bf16[27,32,32]{2,1,0:T(8,128)(2,1)S(1)}, bf16[27,32,32]{2,1,0:T(8,128)(2,1)}, u32[]{:S(2)}) copy-start(bf16[27,32,32]{2,1,0:T(8,128)(2,1)} %param.15) | copy-start | bytes 165892
  2.8 30.4 %copy-start.2 = (bf16[8,32,64]{2,1,0:T(8,128)(2,1)S(1)}, bf16[8,32,64]{2,1,0:T(8,128)(2,1)}, u32[]{:S(2)}) copy-start(bf16[8,32,64]{2,1,0:T(8,128)(2,1)} %w_up.1) | copy-start | bytes 98308
  3.8 29.4 %copy-start.3 = (bf16[27,32]{1,0:T(8,128)(2,1)S(1)}, bf16[27,32]{1,0:T(8,128)(2,1)}, u32[]{:S(2)}) copy-start(bf16[27,32]{1,0:T(8,128)(2,1)} %w_in.1) | copy-start | bytes 5188
  33.2 0.7 copy-start.4
  33.9 1.0 %copy-start = (bf16[27,64,64]{2,1,0:T(8,128)(2,1)S(1)}, bf16[27,64,64]{2,1,0:T(8,128)(2,1)}, u32[]{:S(2)}) copy-start(bf16[27,64,64]{2,1,0:T(8,128)(2,1)} %w_mid.1) | copy-start | bytes 663556

commit v2 on v1

--- a/solution.py
+++ b/solution.py
@@ -37,7 +37,28 @@
 
 
 def spread_kernel(
-    nx, ny, ng, block, halo, full, meta, xg, placed, yr, mine, hr, xs, xr, ys, yw, hs, hw
+    nx,
+    ny,
+    ng,
+    img,
+    tgt,
+    counts,
+    names,
+    halo,
+    full,
+    meta,
+    block,
+    xg,
+    placed,
+    yr,
+    mine,
+    hr,
+    xs,
+    xr,
+    ys,
+    yw,
+    hs,
+    hw,
 ):
     ranks = nx * ny
     g = lax.axis_index("gz")
@@ -48,6 +69,15 @@
     y_peer = [(g, xi * ny + lax.rem(yi + k, ny)) for k in range(ny)]
     around = [(dz, dj) for dz in (0, -1, 1, -2, 2) for dj in (0, -1, 1) if (dz, dj) != (0, 0)]
     near = [(lax.rem(g + dz + ng, ng), lax.rem(j + dj + ranks, ranks)) for dz, dj in around]
+    for s in range(SLOTS):
+        block[s * 32 : s * 32 + 32] = jnp.concatenate(
+            [img[s].astype(F32), tgt[s].astype(F32)], axis=0
+        ).astype(BF16)
+    live = lax.broadcasted_iota(jnp.int32, (1, SLOTS), 1) < counts[...]
+    held = jnp.where(live, names[...], -1).astype(F32)
+    lines = [jnp.broadcast_to(held[:, s : s + 1], (1, 128)) for s in range(SLOTS)]
+    lines.append(jnp.zeros((12, 128), F32))
+    block[128:144] = jnp.concatenate(lines, axis=0).astype(BF16)
     greet(x_peer[1:] + y_peer[1:] + near)
 
     steps = [remote(block, xg.at[k], xs.at[k], xr.at[k], x_peer[k]) for k in range(1, nx)]
@@ -115,7 +145,7 @@
         full[z] = hr[z + 1]
 
 
-def spread_tiles(nx, ny, ng, block):
+def spread_tiles(nx, ny, ng, img, tgt, counts, names):
     return pl.pallas_call(
         functools.partial(spread_kernel, nx, ny, ng),
         out_shape=(
@@ -123,9 +153,10 @@
             jax.ShapeDtypeStruct((3, 4, 32, 128), BF16),
             jax.ShapeDtypeStruct((nx, 16, 128), BF16),
         ),
-        in_specs=[VM],
+        in_specs=[VM] * 4,
         out_specs=(VM, VM, VM),
         scratch_shapes=[
+            pltpu.VMEM((144, 128), BF16),
             pltpu.VMEM((nx, 144, 128), BF16),
             pltpu.VMEM((ny, 2, 32, 128), BF16),
             pltpu.VMEM((ny, 2, 32, 128), BF16),
@@ -142,7 +173,7 @@
             collective_id=0, has_side_effects=True, vmem_limit_bytes=32 << 20
         ),
         name="spread",
-    )(block)
+    )(img, tgt, counts, names)
 
 
 def iota(shape, dim):
@@ -275,7 +306,7 @@
                 at = (zo + dz) * 8 + (xo + dx) * 2 + yo + dy - 1
                 hit = hit | ((tap == t) & (col == at))
         w0[pos * 32 : pos * 32 + 32, :] = dot(taps_t, hot(hit)).astype(BF16)
-    wd_t = jnp.concatenate([dot_t(i32, w_down[tap_of(p)]) for p in range(8)], axis=0).astype(BF16)
+    wd_t = jnp.concatenate([w_down[tap_of(p)] for p in range(8)], axis=0)
     wd = dot_t(i64, wd_t).astype(BF16)
     wu = jnp.concatenate([w_up[tap_of(p)] for p in range(8)], axis=0)
     wu_t = dot_t(i64, wu).astype(BF16)
@@ -351,7 +382,7 @@
         put_fine(c0, 2 * n, h0)
         return carry
 
-    lax.fori_loop(0, 10, first_conv, 0)
+    lax.fori_loop(0, 10, first_conv, 0, unroll=True)
 
     def second_conv(n, carry):
         cols = c0[pl.ds(2 * n + 1, 4)].reshape(1024, wide)
@@ -360,7 +391,7 @@
         put_coarse(cd, n, jnp.maximum(dot(wd, h1), 0.0) * in_slab(n - 3))
         return carry
 
-    lax.fori_loop(0, 8, second_conv, 0)
+    lax.fori_loop(0, 8, second_conv, 0, unroll=True)
 
     def middle(n, carry):
         cols = cd[pl.ds(n, 3)].reshape(768, wide)
@@ -379,7 +410,7 @@
         put_coarse(cg, n, gq)
         return carry
 
-    lax.fori_loop(0, 6, middle, 0)
+    lax.fori_loop(0, 6, middle, 0, unroll=True)
 
     def back(n, carry):
         cols = cg[pl.ds(n, 3)].reshape(768, wide)
@@ -392,7 +423,7 @@
         put_fine(cr, 2 * n, gr)
         return carry
 
-    lax.fori_loop(0, 4, back, 0)
+    lax.fori_loop(0, 4, back, 0, unroll=True)
 
     for n in range(2):
         cols = cr[2 * n + 1 : 2 * n + 5, :, 0:128].reshape(1024, 128)
@@ -440,15 +471,11 @@
             at = MID + (a * 2 + half) * 64
             vec[at : at + 64, :] = dot_t(gq, cols)
     gdd = own(gds, 1)
-    down = dot_t(gdd, own(h1s, 3))
-    vec[DOWN : DOWN + 64, :] = down[:, 0:128]
-    vec[DOWN + 64 : DOWN + 128, :] = down[:, 128:256]
-    gs = own(gss, 2)
-    qq = own(qs, 2)
     none = jnp.zeros((64, 256), BF16)
-    vec[UP : UP + 128, :] = dot_t(gs[0:128], jnp.concatenate([qq, none], axis=0)) + dot_t(
-        gs[128:256], jnp.concatenate([none, qq], axis=0)
-    )
+    for at, fine, coarse in ((DOWN, own(h1s, 3), gdd), (UP, own(gss, 2), own(qs, 2))):
+        vec[at : at + 128, :] = dot_t(
+            fine[0:128], jnp.concatenate([coarse, none], axis=0)
+        ) + dot_t(fine[128:256], jnp.concatenate([none, coarse], axis=0))
     cols = jnp.concatenate([tcol[64:96, 0:128], tcol[80:112, 0:128]], axis=1)
     inp = dot_t(cols, own(gas, 0))
     vec[INP : INP + 32, :] = inp[:, 0:128]
@@ -688,7 +715,8 @@
     )(vec.reshape(CORES, nx, ny, rows, 128), err, meta)
 
 
-def unpack_kernel(vec, g_in, g_res, g_down, g_mid, g_up, g_head, lines):
+def unpack_kernel(vec, tiles, err, g_in, g_res, g_down, g_mid, g_up, g_head, lines):
+    err[...] = tiles[...]
     for zy in range(9):
         strip = vec[RES + zy * 32 : RES + zy * 32 + 32, :]
         for c in range(3):
@@ -706,15 +734,11 @@
             g_mid[t] = jnp.zeros((64, 64), F32)
     for pos in range(8):
         quarter = pos & 3
-        at = DOWN + (pos >> 2) * 64
-        part = vec[at : at + 64, :]
-        if quarter:
-            part = pltpu.roll(part, 128 - 32 * quarter, 1)
-        g_down[tap_of(pos)] = part[:, 0:32]
-        part = vec[UP + quarter * 32 : UP + quarter * 32 + 32, :]
-        if pos >> 2:
-            part = pltpu.roll(part, 64, 1)
-        g_up[tap_of(pos)] = part[:, 0:64]
+        for at, grad in ((DOWN, g_down), (UP, g_up)):
+            part = vec[at + quarter * 32 : at + quarter * 32 + 32, :]
+            if pos >> 2:
+                part = pltpu.roll(part, 64, 1)
+            grad[tap_of(pos)] = part[:, 0:64]
         part = vec[INP + (pos >> 2) * 32 : INP + (pos >> 2) * 32 + 32, :]
         if quarter:
             part = pltpu.roll(part, 128 - 32 * quarter, 1)
@@ -732,23 +756,24 @@
     g_head[...] = vec[HEAD : HEAD + 8, :][0:3, 0:32]
 
 
-def unpack(vec):
+def unpack(vec, tiles):
     return pl.pallas_call(
         unpack_kernel,
         out_shape=(
+            jax.ShapeDtypeStruct((96, 128), BF16),
             jax.ShapeDtypeStruct((27, 32), F32),
             jax.ShapeDtypeStruct((27, 32, 32), F32),
-            jax.ShapeDtypeStruct((8, 64, 32), F32),
+            jax.ShapeDtypeStruct((8, 32, 64), F32),
             jax.ShapeDtypeStruct((27, 64, 64), F32),
             jax.ShapeDtypeStruct((8, 32, 64), F32),
             jax.ShapeDtypeStruct((3, 32), F32),
         ),
-        in_specs=[VM],
-        out_specs=(VM,) * 6,
+        in_specs=[VM] * 2,
+        out_specs=(VM,) * 7,
         scratch_shapes=[pltpu.VMEM((8, 32, 128), F32)],
         compiler_params=pltpu.CompilerParams(vmem_limit_bytes=32 << 20),
         name="unpack",
-    )(vec)
+    )(vec, tiles)
 
 
 def local(
@@ -757,19 +782,15 @@
     ranks = lax.axis_size("xy")
     ng = lax.axis_size("gz")
     nx, ny = grid_of(ranks)
-    live = jnp.arange(SLOTS) < owner_counts[0, 0]
-    names = jnp.where(live, tile_list[0, 0], -1).astype(BF16)
-    names = jnp.broadcast_to(jnp.pad(names, (0, 12))[:, None], (16, 128))
-    block = jnp.concatenate(
-        [
-            jnp.concatenate(
-                [tile_image.reshape(SLOTS, 8, 128), tile_target.reshape(SLOTS, 24, 128)], axis=1
-            ).reshape(SLOTS * 32, 128),
-            names,
-        ],
-        axis=0,
+    halo, full, meta = spread_tiles(
+        nx,
+        ny,
+        ng,
+        tile_image.reshape(SLOTS, 8, 128),
+        tile_target.reshape(SLOTS, 24, 128),
+        owner_counts,
+        tile_list.reshape(1, SLOTS),
     )
-    halo, full, meta = spread_tiles(nx, ny, ng, block)
     vec, err = local_step(
         2 * ng,
         128 * ranks,
@@ -778,14 +799,15 @@
         full,
         w_in,
         w_res.reshape(9, 3, 32, 32),
-        w_down,
+        jnp.transpose(w_down, (0, 2, 1)),
         w_mid,
         w_up,
         head_weight,
     )
     sums, tiles = sum_all(nx, ny, ng // CORES, vec, err, meta)
-    grads = unpack(sums.reshape(ROWS, 128))
-    return (tiles.reshape(1, 1, SLOTS, 3, 4, 2, 128),) + tuple(grads)
+    tiles, g_in, g_res, g_down, g_mid, g_up, g_head = unpack(sums.reshape(ROWS, 128), tiles)
+    tiles = tiles.reshape(1, 1, SLOTS, 3, 4, 2, 128)
+    return (tiles, g_in, g_res, jnp.transpose(g_down, (0, 2, 1)), g_mid, g_up, g_head)
 
 
 def solution(mesh):

time: 88.7 us -> 83.3 us (0.939)
  Pallas kernels: 81.4 us -> 75.8 us
  local copies, waits for them, and re-layouts: 4.05 us -> 5.68 us
  other arithmetic: 1.5 us -> 0 us
    pallas_call x1, Pallas kernels: 18.2 us -> 12.4 us  [local_step(): pl.pallas_call(functools.partial(step_kernel, nz, nx_cells, float(voxels)...]
    unnamed x13 -> x18, local copies, waits for them, and re-layouts: 4.05 us -> 5.68 us
where the time goes in v2:
time: 83.3 us; the launch traced here: 82.8 us
  Pallas kernels  75.8 us (91%)
  local copies, waits for them, and re-layouts  5.68 us (7%)
  between operations  1.35 us (2%)
    pallas_call x1, Pallas kernels, sum_all(): pl.pallas_call(functools.partial(sum_kernel, nx, ny, nzc), out_shape=(jax...  32.6 us
    pallas_call x1, Pallas kernels, spread_tiles(): pl.pallas_call(functools.partial(spread_kernel, nx, ny, ng), out_shape=(j...  29.4 us
    pallas_call x1, Pallas kernels, local_step(): pl.pallas_call(functools.partial(step_kernel, nz, nx_cells, float(voxels)...  12.4 us
    unnamed x18, local copies, waits for them, and re-layouts  5.68 us

profile of v2, /device:TPU:1, one launch (start us, length us, event | category | flops | bytes accessed | tf_op | source)
XLA Modules:
  0.0 82.8 jit_solution(14968580299611083706)
XLA Ops:
  0.6 0.0 copy-start.6
  1.3 0.0 copy-start.8
  1.3 0.0 copy-done.6
  1.3 0.6 copy-done.8
  2.0 0.0 copy-start.4
  2.0 0.7 copy-done.4
  2.7 0.0 copy-start.5
  2.7 29.4 %spread.1 = (bf16[5,4,16,128]{3,2,1,0:T(8,128)(2,1)S(1)}, bf16[3,4,32,128]{3,2,1,0:T(8,128)(2,1)S(1)}, bf16[4,16,128]{2,1,0:T(8,128)(2,1)S(1)}) custom-call(bf16[4,8,128]{2,1,0:T(8,128)(2,1)S(1)} %bitcast.14, bf16[4,24,128]{2,1,0:T(8,128)(2,1)S(1)} %bitcast.13, s32[1,1]{1,0:T(1,128)S(6)} %copy.17.counts, s32[1,4]{1,0:T(1,128)S(1)} %bitcast.15), custom_call_target="tpu_custom_call" | custom-call | tf_op jit(solution)/shard_map/spread/pallas_call | solution.py:149
  32.1 0.0 copy-start.7
  32.1 0.0 copy-done.5
  32.1 0.7 copy-done.7
  32.8 0.0 copy-start
  32.8 1.0 %copy-done = bf16[27,64,64]{2,1,0:T(8,128)(2,1)S(1)} copy-done((bf16[27,64,64]{2,1,0:T(8,128)(2,1)S(1)}, bf16[27,64,64]{2,1,0:T(8,128)(2,1)}, u32[]{:S(2)}) %copy-start) | copy-done | bytes 221208
  33.8 0.0 copy-start.1
  33.8 0.9 %copy-done.1 = bf16[27,32,32]{2,1,0:T(8,128)(2,1)S(1)} copy-done((bf16[27,32,32]{2,1,0:T(8,128)(2,1)S(1)}, bf16[27,32,32]{2,1,0:T(8,128)(2,1)}, u32[]{:S(2)}) %copy-start.1) | copy-done | bytes 55320
  34.7 0.0 copy-start.2
  34.7 0.8 %copy-done.2 = bf16[8,64,32]{1,2,0:T(8,128)(2,1)S(1)} copy-done((bf16[8,64,32]{1,2,0:T(8,128)(2,1)S(1)}, bf16[8,64,32]{1,2,0:T(8,128)(2,1)}, u32[]{:S(2)}) %copy-start.2) | copy-done | bytes 32792
  35.6 0.0 copy-start.3
  35.6 0.8 %copy-done.3 = bf16[8,32,64]{2,1,0:T(8,128)(2,1)S(1)} copy-done((bf16[8,32,64]{2,1,0:T(8,128)(2,1)S(1)}, bf16[8,32,64]{2,1,0:T(8,128)(2,1)}, u32[]{:S(2)}) %copy-start.3) | copy-done | bytes 32792
  36.4 12.4 %step.1 = (f32[1024,128]{1,0:T(8,128)S(1)}, bf16[48,128]{1,0:T(8,128)(2,1)S(1)}) custom-call(bf16[5,4,16,128]{3,2,1,0:T(8,128)(2,1)S(1)} %get-tuple-element.21.halo, bf16[3,4,32,128]{3,2,1,0:T(8,128)(2,1)S(1)} %get-tuple-element.22.full, bf16[27,32]{1,0:T(8,128)(2,1)S(1)} %copy-done.5, bf16[9,3,32,32]{3,2,1,0:T(8,128)(2,1)S(1)} %bitcast.11, ...), custom_call_target="tpu_custom_call" | custom-call | tf_op jit(solution)/shard_map/step/pallas_call | solution.py:495
  48.8 32.6 %sums.1 = (f32[2,4,8,16,128]{4,3,2,1,0:T(8,128)S(1)}, bf16[96,128]{1,0:T(8,128)(2,1)S(1)}) custom-call(f32[2,4,8,16,128]{4,3,2,1,0:T(8,128)S(1)} %bitcast.10, bf16[48,128]{1,0:T(8,128)(2,1)S(1)} %get-tuple-element.24.err, bf16[4,16,128]{2,1,0:T(8,128)(2,1)S(1)} %get-tuple-element.25.meta), custom_call_target="tpu_custom_call" | custom-call | tf_op jit(solution)/shard_map/sums/pallas_call | solution.py:680
  81.5 1.4 %unpack.1 = (bf16[96,128]{1,0:T(8,128)(2,1)}, f32[27,32]{1,0:T(8,128)}, f32[27,32,32]{2,1,0:T(8,128)}, f32[8,32,64]{2,1,0:T(8,128)}, f32[27,64,64]{2,1,0:T(8,128...) custom-call(f32[1024,128]{1,0:T(8,128)S(1)} %bitcast.9, bf16[96,128]{1,0:T(8,128)(2,1)S(1)} %get-tuple-element.27.tiles), custom_call_target="tpu_custom_call" | custom-call | tf_op jit(solution)/shard_map/unpack/pallas_call | solution.py:760
Async XLA Ops:
  0.6 0.7 copy-start.6
  1.3 0.7 copy-start.8
  2.0 0.7 copy-start.4
  2.7 29.4 %copy-start.5 = (bf16[27,32]{1,0:T(8,128)(2,1)S(1)}, bf16[27,32]{1,0:T(8,128)(2,1)}, u32[]{:S(2)}) copy-start(bf16[27,32]{1,0:T(8,128)(2,1)} %w_in.1) | copy-start | bytes 5188
  32.1 0.7 copy-start.7
  32.8 1.0 %copy-start = (bf16[27,64,64]{2,1,0:T(8,128)(2,1)S(1)}, bf16[27,64,64]{2,1,0:T(8,128)(2,1)}, u32[]{:S(2)}) copy-start(bf16[27,64,64]{2,1,0:T(8,128)(2,1)} %w_mid.1) | copy-start | bytes 663556
  33.8 0.9 %copy-start.1 = (bf16[27,32,32]{2,1,0:T(8,128)(2,1)S(1)}, bf16[27,32,32]{2,1,0:T(8,128)(2,1)}, u32[]{:S(2)}) copy-start(bf16[27,32,32]{2,1,0:T(8,128)(2,1)} %param.15) | copy-start | bytes 165892
  34.7 0.8 %copy-start.2 = (bf16[8,64,32]{1,2,0:T(8,128)(2,1)S(1)}, bf16[8,64,32]{1,2,0:T(8,128)(2,1)}, u32[]{:S(2)}) copy-start(bf16[8,64,32]{1,2,0:T(8,128)(2,1)} %param.16) | copy-start | bytes 98308
  35.6 0.8 %copy-start.3 = (bf16[8,32,64]{2,1,0:T(8,128)(2,1)S(1)}, bf16[8,32,64]{2,1,0:T(8,128)(2,1)}, u32[]{:S(2)}) copy-start(bf16[8,32,64]{2,1,0:T(8,128)(2,1)} %w_up.1) | copy-start | bytes 98308

commit v3 on v0

v3 whole, which is shorter than its diff:
```python
import functools
import types

import jax
import jax.numpy as jnp
from jax import lax
from jax.experimental import pallas as pl
from jax.experimental.pallas import tpu as pltpu
from jax.sharding import PartitionSpec as P

F32 = jnp.float32
BF16 = jnp.bfloat16
MESH = pl.DeviceIdType.MESH
SLOTS = 4
CORES = 2
ROWS = 1024
VM = pl.BlockSpec(memory_space=pltpu.VMEM)

RES, MID, DOWN, UP, INP, HEAD, USED = 0, 288, 672, 800, 928, 992, 1000


def grid_of(ranks):
    height = 8 if ranks == 32 else 2
    return ranks // height, height


def remote(src, dst, send, recv, where):
    return pltpu.make_async_remote_copy(
        src_ref=src, dst_ref=dst, send_sem=send, recv_sem=recv, device_id=where, device_id_type=MESH
    )


def iota(shape, dim):
    return lax.broadcasted_iota(jnp.int32, shape, dim)


def dot(a, b):
    return jnp.dot(a, b, preferred_element_type=F32)


def dot_t(a, b):
    return lax.dot_general(a, b, (((1,), (1,)), ((), ())), preferred_element_type=F32)


def hot(cond):
    return jnp.where(cond, 1.0, 0.0).astype(BF16)


def eye(n):
    return hot(iota((n, n), 0) == iota((n, n), 1))


def before(v):
    return pltpu.roll(v, 1, 1)


def after(v):
    return pltpu.roll(v, v.shape[1] - 1, 1)


def put_fine(buf, at, v):
    prev = before(v[128:256]).astype(BF16)
    succ = after(v[0:128]).astype(BF16)
    even = v[0:128].astype(BF16)
    odd = v[128:256].astype(BF16)
    for zo in range(2):
        for yo in range(2):
            rows = slice(zo * 64 + yo * 32, zo * 64 + yo * 32 + 32)
            for n, part in enumerate((prev, even, odd, succ)):
                buf[at + zo, yo * 128 + n * 32 : yo * 128 + n * 32 + 32, :] = part[rows]


def put_coarse(buf, at, v):
    buf[at, 0:64, :] = before(v).astype(BF16)
    buf[at, 64:128, :] = v.astype(BF16)
    buf[at, 128:192, :] = after(v).astype(BF16)
    buf[at, 192:256, :] = jnp.zeros((64, v.shape[1]), BF16)


def tap_of(pos):
    return (pos >> 1 & 1) * 4 + (pos & 1) * 2 + (pos >> 2)


def whole_kernel(nx, ny, ng, names, *refs):
    r = types.SimpleNamespace(**dict(zip(names, refs)))
    ranks = nx * ny
    nzc = ng // CORES
    nz = 2 * ng
    nx_cells = 128 * ranks
    voxels = float(ng * ranks * 2048)
    wide = 256
    g = lax.axis_index("gz")
    j = lax.axis_index("xy")
    xi = j // ny
    yi = lax.rem(j, ny)
    zi = g // CORES
    core = lax.rem(g, CORES)
    other = (zi * CORES + 1 - core, j)
    x_at = [lax.rem(xi + k, nx) for k in range(nx)]
    y_at = [lax.rem(yi + k, ny) for k in range(ny)]
    x_peer = [(g, x_at[k] * ny + yi) for k in range(nx)]
    y_peer = [(g, xi * ny + y_at[k]) for k in range(ny)]
    z_peer = [(lax.rem(zi + k, nzc) * CORES + core, j) for k in range(nzc)]
    around = [(dz, dj) for dz in (0, -1, 1, -2, 2) for dj in (0, -1, 1) if (dz, dj) != (0, 0)]
    near = [(lax.rem(g + dz + ng, ng), lax.rem(j + dj + ranks, ranks)) for dz, dj in around]

    moves = (
        (r.tile_list, r.list_v),
        (r.counts, r.count_v),
        (r.img, r.xgi.at[0]),
        (r.target, r.xgt.at[0]),
        (r.w_res, r.w_res_v),
        (r.w_mid, r.w_mid_v),
        (r.w_down, r.w_down_v),
        (r.w_up, r.w_up_v),
        (r.w_in, r.w_in_v),
        (r.head, r.head_v),
    )
    loads = [pltpu.make_async_copy(src, dst, r.loaded.at[n]) for n, (src, dst) in enumerate(moves)]
    for copy in loads:
        copy.start()
    barrier = pltpu.get_barrier_semaphore()
    peers = [other] + x_peer[1:] + y_peer[1:] + z_peer[1:] + near
    for peer in peers:
        pl.semaphore_signal(barrier, inc=1, device_id=peer, device_id_type=MESH)
    for copy in loads[0:2]:
        copy.wait()
    live = lax.broadcasted_iota(jnp.int32, (1, SLOTS), 1) < r.count_v[...]
    held = jnp.where(live, r.list_v[...], -1).astype(F32)
    lines = [jnp.broadcast_to(held[:, s : s + 1], (1, 128)) for s in range(SLOTS)]
    lines.append(jnp.zeros((12, 128), F32))
    r.meta[0] = jnp.concatenate(lines, axis=0).astype(BF16)
    pl.semaphore_wait(barrier, len(peers))

    name_x = [
        remote(r.meta.at[0], r.meta.at[k], r.s_name.at[k], r.r_name.at[k], x_peer[k])
        for k in range(1, nx)
    ]
    img_x = [
        remote(r.img, r.xgi.at[k], r.s_ix.at[k], r.r_ix.at[k], x_peer[k]) for k in range(1, nx)
    ]
    tgt_x = [
        remote(r.target, r.xgt.at[k], r.s_tx.at[k], r.r_tx.at[k], x_peer[k]) for k in range(1, nx)
    ]
    for copy in name_x + img_x + tgt_x:
        copy.start()
    for copy in loads[4:]:
        copy.wait()

    i32, i64 = eye(32), eye(64)
    for xo in range(2):
        fwd = jnp.zeros((288, 128), F32)
        for c in range(3):
            put = hot(iota((32, 128), 1) == iota((32, 128), 0) + 32 * (c + xo))
            fwd = fwd + dot(r.w_res_v[:, c].reshape(288, 32), put)
        fwd = fwd.astype(BF16)
        blank = jnp.zeros((32, 32), BF16)
        for zy in range(9):
            parts = [r.w_res_v[8 - zy, 2 - c] for c in range(3)]
            parts = [blank] + parts if xo else parts + [blank]
            bwd = dot_t(i32, jnp.concatenate(parts, axis=0)).astype(BF16)
            dz, dy = zy // 3, zy % 3
            for zo in range(2):
                for yo in range(2):
                    y_in = yo + dy - 1
                    if 0 <= y_in < 2:
                        rows = slice(xo * 128 + zo * 64 + yo * 32, xo * 128 + zo * 64 + yo * 32 + 32)
                        lanes = slice((zo + dz) * 256 + y_in * 128, (zo + dz) * 256 + y_in * 128 + 128)
                        r.w1[rows, lanes] = fwd[zy * 32 : zy * 32 + 32]
                        r.w1b[rows, lanes] = bwd
        for zo in range(2):
            for yo in range(2):
                rows = slice(xo * 128 + zo * 64 + yo * 32, xo * 128 + zo * 64 + yo * 32 + 32)
                lanes = slice((3 - 3 * zo) * 256, (3 - 3 * zo) * 256 + 256)
                r.w1[rows, lanes] = jnp.zeros((32, 256), BF16)
                r.w1b[rows, lanes] = jnp.zeros((32, 256), BF16)
    taps_t = dot_t(i32, r.w_in_v[...]).astype(BF16)
    col = iota((27, 32), 1)
    tap = iota((27, 32), 0)
    for pos in range(8):
        xo, zo, yo = pos >> 2, pos >> 1 & 1, pos & 1
        hit = jnp.zeros((27, 32), jnp.bool_)
        for t in range(27):
            dz, dy, dx = t // 9, t // 3 % 3, t % 3
            if 0 <= yo + dy - 1 < 2:
                at = (zo + dz) * 8 + (xo + dx) * 2 + yo + dy - 1
                hit = hit | ((tap == t) & (col == at))
        r.w0[pos * 32 : pos * 32 + 32, :] = dot(taps_t, hot(hit)).astype(BF16)
    wd_t = jnp.concatenate([r.w_down_v[tap_of(p)] for p in range(8)], axis=0)
    wd = dot_t(i64, wd_t).astype(BF16)
    wu = jnp.concatenate([r.w_up_v[tap_of(p)] for p in range(8)], axis=0)
    wu_t = dot_t(i64, wu).astype(BF16)
    blank = jnp.zeros((64, 64), BF16)
    for a in range(3):
        fwd = [dot_t(i64, r.w_mid_v[9 * a + 3 + c]).astype(BF16) for c in range(3)] + [blank]
        bwd = [r.w_mid_v[26 - (9 * a + 3 + c)] for c in range(3)] + [blank]
        r.wm[:, a * 256 : a * 256 + 256] = dot_t(i64, jnp.concatenate(fwd, axis=0)).astype(BF16)
        r.wmb[:, a * 256 : a * 256 + 256] = dot_t(i64, jnp.concatenate(bwd, axis=0)).astype(BF16)
    heads = dot(r.head_v[...], hot((iota((32, 256), 1) & 31) == iota((32, 256), 0)))
    hd = jnp.concatenate(
        [jnp.broadcast_to(heads[a : a + 1], (8, 256)) for a in range(3)]
        + [jnp.zeros((8, 256), F32)],
        axis=0,
    )
    same = (iota((32, 256), 0) & 7) == (iota((32, 256), 1) >> 5)
    hd = jnp.where(same, hd, 0.0).astype(BF16)
    hd_t = dot_t(eye(256), hd).astype(BF16)


    for copy in [loads[2]]:
        copy.wait()
    for copy in name_x + img_x:
        copy.wait_recv()

    def select(k, tiles, rows):
        first = ((xi * ny + lax.rem(yi + k, ny)) * 2).astype(F32)
        sums = [jnp.zeros((rows, 128), F32), jnp.zeros((rows, 128), F32)]
        for a in range(nx):
            called = r.meta[a].astype(F32)
            held = tiles[a].astype(F32)
            for s in range(SLOTS):
                tile = held[s * rows : s * rows + rows]
                for t in range(2):
                    sums[t] = sums[t] + jnp.where(called[s : s + 1] == first + t, tile, 0.0)
        return jnp.concatenate(sums, axis=0).astype(BF16)

    def img_y(k):
        peer = (g, xi * ny + lax.rem(yi + k, ny))
        return remote(r.pli.at[k], r.yri.at[k], r.s_iy.at[k], r.r_iy.at[k], peer)

    def tgt_y(k):
        peer = (g, xi * ny + lax.rem(yi + k, ny))
        return remote(r.plt.at[k], r.yrt.at[k], r.s_ty.at[k], r.r_ty.at[k], peer)

    def send_img(k, carry):
        r.pli[k] = select(k, r.xgi, 8)
        img_y(k).start()
        return carry

    def send_tgt(k, carry):
        r.plt[k] = select(k, r.xgt, 24)
        tgt_y(k).start()
        return carry

    lax.fori_loop(1, ny, send_img, 0)
    loads[3].wait()
    for copy in tgt_x:
        copy.wait_recv()
    lax.fori_loop(1, ny, send_tgt, 0)
    r.pli[0] = select(0, r.xgi, 8)
    r.plt[0] = select(0, r.xgt, 24)

    total = r.pli[0].astype(F32)
    for k in range(1, ny):
        img_y(k).wait_recv()
        total = total + r.yri[k].astype(F32)
    r.mi[...] = total.astype(BF16)
    img_n = [
        remote(r.mi, r.hri.at[2 - dz, 1 - dj], r.s_in.at[n], r.r_in.at[n], near[n])
        for n, (dz, dj) in enumerate(around)
    ]
    for copy in img_n:
        copy.start()
    r.hri[2, 1] = r.mi[...]
    total = r.plt[0].astype(F32)
    for k in range(1, ny):
        tgt_y(k).wait_recv()
        total = total + r.yrt[k].astype(F32)
    r.mt[...] = total.astype(BF16)
    tgt_n = [
        remote(r.mt, r.hrt.at[1 - dz, 1 - dj], r.s_tn.at[n], r.r_tn.at[n], near[n])
        for n, (dz, dj) in enumerate(around)
        if abs(dz) < 2
    ]
    for copy in tgt_n:
        copy.start()
    r.hrt[1, 1] = r.mt[...]
    for copy in img_n:
        copy.wait_recv()

    def wide_rows(ref, z, rows):
        left, own, right = (ref[z, n].astype(F32) for n in range(3))
        return jnp.concatenate([left[rows:], own[:rows], own[rows:], right[:rows]], axis=1)

    image = jnp.concatenate([wide_rows(r.hri, z, 8) for z in range(5)], axis=0)
    z2 = iota((40, 512), 0) + 8 * g - 16
    x1 = iota((40, 512), 1) + 256 * j - 128
    inside = (z2 >= 0) & (z2 < 4 * nz) & (x1 >= 0) & (x1 < 2 * nx_cells)
    image = jnp.where(inside, image, 0.0).astype(BF16)
    place = iota((512, wide), 0)
    lane2 = 2 * iota((512, wide), 1) + 128
    pick = [hot(place == ((lane2 + k) & 511)) for k in (-1, 0, 1, 2)]
    parts = jnp.concatenate([dot(image, p) for p in pick], axis=0).astype(BF16)
    row = iota((176, 160), 0)
    zrow = row >> 3
    source = ((row >> 1) & 3) * 40 + (zrow - 1) * 2 + (row & 1)
    order = hot((iota((176, 160), 1) == source) & (zrow >= 1) & (zrow <= 20))
    r.tcol[...] = dot(order, parts).astype(BF16)

    lane = iota((1, wide), 1)
    cell = jnp.where(lane < 192, lane, lane - 256) + 128 * j
    lane_in = jnp.where((cell >= 0) & (cell < nx_cells), 1.0, 0.0)

    def in_slab(zc):
        at = 2 * g + zc
        return lane_in * jnp.where((at >= 0) & (at < nz), 1.0, 0.0)

    def first_conv(n, carry):
        rows = r.tcol[pl.ds(pl.multiple_of(n * 16, 16), 32), :]
        h0 = jnp.maximum(dot(r.w0[...], rows), 0.0) * in_slab(n - 4)
        r.h0s[n] = h0.astype(BF16)
        put_fine(r.c0, 2 * n, h0)
        return carry

    lax.fori_loop(0, 10, first_conv, 0, unroll=True)

    def second_conv(n, carry):
        cols = r.c0[pl.ds(2 * n + 1, 4)].reshape(1024, wide)
        h1 = jnp.maximum(r.h0s[n + 1].astype(F32) + dot(r.w1[...], cols), 0.0).astype(BF16)
        r.h1s[n] = h1
        put_coarse(r.cd, n, jnp.maximum(dot(wd, h1), 0.0) * in_slab(n - 3))
        return carry

    lax.fori_loop(0, 8, second_conv, 0, unroll=True)


    for copy in tgt_n:
        copy.wait_recv()
    target = jnp.concatenate([wide_rows(r.hrt, z, 24) for z in range(3)], axis=0).astype(BF16)
    parts = jnp.concatenate([dot(target, p) for p in pick[1:3]], axis=0).astype(BF16)
    row = iota((192, 144), 0)
    source = (
        ((row >> 2) & 1) * 72
        + (row >> 6) * 24
        + ((row >> 3) & 3) * 8
        + (((row >> 5) & 1) * 2 + ((row >> 1) & 1)) * 2
        + (row & 1)
    )
    order = hot((iota((192, 144), 1) == source) & (((row >> 3) & 3) < 3))
    placed = dot(order, parts)
    for n in range(6):
        r.tgt[n] = placed[n * 32 : n * 32 + 32]


    def middle(n, carry):
        cols = r.cd[pl.ds(n, 3)].reshape(768, wide)
        q = jnp.maximum(r.cd[n + 1, 64:128].astype(F32) + dot(r.wm[...], cols), 0.0).astype(BF16)
        r.qs[n] = q
        s = jnp.maximum(r.h1s[n + 1].astype(F32) + dot(wu, q), 0.0).astype(BF16)
        r.ss[n] = s
        aff = jax.nn.sigmoid(dot(hd, s))
        err = aff - r.tgt[n]
        r.errs[n] = err.astype(BF16)
        gl = (err * aff * (1.0 - aff) / voxels).astype(BF16)
        r.gls[n] = gl
        gs = jnp.where(s.astype(F32) > 0, dot(hd_t, gl), 0.0).astype(BF16)
        r.gss[n] = gs
        gq = jnp.where(q.astype(F32) > 0, dot(wu_t, gs), 0.0) * in_slab(n - 2)
        put_coarse(r.cg, n, gq)
        return carry

    lax.fori_loop(0, 6, middle, 0, unroll=True)


    def own(ref, first):
        return jnp.concatenate([ref[first, :, 0:128], ref[first + 1, :, 0:128]], axis=1)


    rows = jnp.concatenate([r.errs[2, :, 0:128], r.errs[3, :, 0:128]], axis=0)
    src = iota((128, 256), 0)
    dst = iota((128, 256), 1)
    parts = jnp.concatenate([dot(rows, hot(dst == 2 * src + xo)) for xo in range(2)], axis=0)
    row = iota((32, 128), 0)
    source = ((row >> 2) & 1) * 32 + (row >> 3) * 8 + ((row >> 1) & 1) * 2 + (row & 1)
    q = iota((32, 128), 1)
    order = hot((q == source) | (q == source + 68))
    tiles = dot(order, parts.astype(BF16))
    r.err[...] = jnp.concatenate([tiles[0:24, 0:128], tiles[0:24, 128:256]], axis=0).astype(BF16)


    err_y = [remote(r.err, r.ey.at[k], r.s_ey.at[k], r.r_ey.at[k], y_peer[k]) for k in range(1, ny)]
    for copy in err_y:
        copy.start()
    r.ey[0] = r.err[...]

    def back(n, carry):
        cols = r.cg[pl.ds(n, 3)].reshape(768, wide)
        gdd = r.cg[n + 1, 64:128].astype(F32) + dot(r.wmb[...], cols)
        gdd = jnp.where(r.cd[n + 2, 64:128].astype(F32) > 0, gdd, 0.0).astype(BF16)
        r.gds[n] = gdd
        gr = r.gss[n + 1].astype(F32) + dot(wd_t, gdd)
        gr = jnp.where(r.h1s[n + 2].astype(F32) > 0, gr, 0.0) * in_slab(n - 1)
        r.grs[n] = gr.astype(BF16)
        put_fine(r.cr, 2 * n, gr)
        return carry

    lax.fori_loop(0, 4, back, 0, unroll=True)

    for n in range(2):
        cols = r.cr[2 * n + 1 : 2 * n + 5, :, 0:128].reshape(1024, 128)
        ga = r.grs[n + 1, :, 0:128].astype(F32) + dot(r.w1b[...], cols)
        r.gas[n] = jnp.where(r.h0s[n + 4, :, 0:128].astype(F32) > 0, ga, 0.0).astype(BF16)


    gr = own(r.grs, 1)
    for z_in in range(4):
        for y_in in range(2):
            lanes = slice(y_in * 128, y_in * 128 + 128)
            cols = jnp.concatenate([r.c0[7 + z_in, lanes, 0:128], r.c0[9 + z_in, lanes, 0:128]], axis=1)
            part = dot_t(gr, cols)
            for zo in range(2):
                for yo in range(2):
                    dz, dy = z_in - zo, y_in - yo + 1
                    if 0 <= dz < 3:
                        rows = zo * 64 + yo * 32
                        both = part[rows : rows + 32] + pltpu.roll(
                            part[128 + rows : 128 + rows + 32], 96, 1
                        )
                        at = RES + (dz * 3 + dy) * 32
                        if z_in == dz and y_in == max(dy - 1, 0):
                            r.vec[at : at + 32, :] = both
                        else:
                            r.vec[at : at + 32, :] += both
    gq = jnp.concatenate([r.cg[2, 64:128, 0:128], r.cg[3, 64:128, 0:128]], axis=1)
    for a in range(3):
        for half in range(2):
            lanes = slice(half * 128, half * 128 + 128)
            cols = jnp.concatenate([r.cd[2 + a, lanes, 0:128], r.cd[3 + a, lanes, 0:128]], axis=1)
            at = MID + (a * 2 + half) * 64
            r.vec[at : at + 64, :] = dot_t(gq, cols)
    gdd = own(r.gds, 1)
    none = jnp.zeros((64, 256), BF16)
    for at, fine, coarse in ((DOWN, own(r.h1s, 3), gdd), (UP, own(r.gss, 2), own(r.qs, 2))):
        r.vec[at : at + 128, :] = dot_t(
            fine[0:128], jnp.concatenate([coarse, none], axis=0)
        ) + dot_t(fine[128:256], jnp.concatenate([none, coarse], axis=0))
    cols = jnp.concatenate([r.tcol[64:96, 0:128], r.tcol[80:112, 0:128]], axis=1)
    inp = dot_t(cols, own(r.gas, 0))
    r.vec[INP : INP + 32, :] = inp[:, 0:128]
    r.vec[INP + 32 : INP + 64, :] = inp[:, 128:256]
    heads = jnp.where(same, dot_t(own(r.gls, 2), own(r.ss, 2)), 0.0)
    r.vec[HEAD:ROWS, :] = jnp.zeros((ROWS - HEAD, 128), F32)
    for a in range(3):
        line = jnp.sum(heads[a * 8 : a * 8 + 8], axis=0, keepdims=True)
        line = line[:, 0:128] + line[:, 128:256]
        line = line + pltpu.roll(line, 64, 1)
        line = line + pltpu.roll(line, 32, 1)
        r.vec[HEAD + a : HEAD + a + 1, :] = line


    half = ROWS // CORES
    rows_x = half // nx
    rows_y = rows_x // ny

    def piece(k, size):
        return pl.ds(pl.multiple_of(k * size, size), size)

    swap = remote(r.vec.at[piece(1 - core, half)], r.rc, r.s_c.at[0], r.r_c.at[0], other)
    swap.start()
    for copy in err_y:
        copy.wait_recv()

    def answer(a, carry):
        called = r.meta[a].astype(F32)
        sums = [jnp.zeros((24, 128), F32) for _ in range(SLOTS)]
        for k in range(ny):
            first = ((xi * ny + lax.rem(yi - k + ny, ny)) * 2).astype(F32)
            pair = r.ey[k].astype(F32)
            for t in range(2):
                for s in range(SLOTS):
                    sums[s] = sums[s] + jnp.where(
                        called[s : s + 1] == first + t, pair[t * 24 : t * 24 + 24], 0.0
                    )
        r.em[a] = jnp.concatenate(sums, axis=0).astype(BF16)
        return carry

    lax.fori_loop(0, nx, answer, 0)
    swap.wait_recv()
    r.ac[...] = r.vec[piece(core, half), :] + r.rc[...]
    over_x = [
        remote(r.ac.at[piece(x_at[k], rows_x)], r.rx.at[k], r.s_x.at[k], r.r_x.at[k], x_peer[k])
        for k in range(1, nx)
    ]
    err_x = [
        remote(r.em.at[nx - k], r.ex.at[k], r.s_ex.at[k], r.r_ex.at[k], x_peer[k])
        for k in range(1, nx)
    ]
    for copy in over_x + err_x:
        copy.start()
    for copy in over_x:
        copy.wait_recv()
    total = r.ac[piece(xi, rows_x), :]
    for k in range(1, nx):
        total = total + r.rx[k]
    r.ax[...] = total
    over_y = [
        remote(r.ax.at[piece(y_at[k], rows_y)], r.ry.at[k], r.s_y.at[k], r.r_y.at[k], y_peer[k])
        for k in range(1, ny)
    ]
    for copy in over_y:
        copy.start()
    for copy in over_y:
        copy.wait_recv()
    total = r.ax[piece(yi, rows_y), :]
    for k in range(1, ny):
        total = total + r.ry[k]
    r.ay[...] = total
    over_z = [remote(r.ay, r.rz.at[zi], r.s_z.at[k], r.r_z.at[k], z_peer[k]) for k in range(1, nzc)]
    for copy in over_z:
        copy.start()
    r.rz[zi] = r.ay[...]
    for k in range(1, nzc):
        at = lax.rem(zi - k + nzc, nzc)
        remote(r.ay, r.rz.at[at], r.s_z.at[k], r.r_z.at[k], z_peer[k]).wait_recv()
    total = r.rz[0]
    for k in range(1, nzc):
        total = total + r.rz[k]
    r.gy[yi] = total
    back_y = [
        remote(r.gy.at[yi], r.gy.at[yi], r.s_gy.at[k], r.r_gy.at[k], y_peer[k])
        for k in range(1, ny)
    ]
    for copy in back_y:
        copy.start()
    for k in range(1, ny):
        at = lax.rem(yi - k + ny, ny)
        remote(r.gy.at[at], r.gy.at[at], r.s_gy.at[k], r.r_gy.at[k], y_peer[k]).wait_recv()
    r.gx[xi] = r.gy[...].reshape(rows_x, 128)
    back_x = [
        remote(r.gx.at[xi], r.gx.at[xi], r.s_gx.at[k], r.r_gx.at[k], x_peer[k])
        for k in range(1, nx)
    ]
    for copy in back_x:
        copy.start()
    for k in range(1, nx):
        at = lax.rem(xi - k + nx, nx)
        remote(r.gx.at[at], r.gx.at[at], r.s_gx.at[k], r.r_gx.at[k], x_peer[k]).wait_recv()
    back_c = remote(r.gx, r.gc, r.s_c.at[1], r.r_c.at[1], other)
    back_c.start()
    r.out[piece(core, half), :] = r.gx[...].reshape(half, 128)
    for copy in err_x:
        copy.wait_recv()
    total = r.em[0].astype(F32)
    for k in range(1, nx):
        total = total + r.ex[k].astype(F32)
    r.tiles[...] = total.astype(BF16)
    back_c.wait_recv()
    r.out[piece(1 - core, half), :] = r.gc[...].reshape(half, 128)
    sent = [swap, back_c] + name_x + img_x + tgt_x + img_n + tgt_n + err_y + err_x
    sent += [img_y(k) for k in range(1, ny)] + [tgt_y(k) for k in range(1, ny)]
    for copy in sent + over_x + over_y + over_z + back_y + back_x:
        copy.wait_send()


def whole(nx, ny, ng, operands):
    wide = 256
    nzc = ng // CORES
    half = ROWS // CORES
    rows_x = half // nx
    rows_y = rows_x // ny
    buffers = dict(
        list_v=((1, SLOTS), jnp.int32),
        count_v=((1, 1), jnp.int32),
        w_res_v=((9, 3, 32, 32), BF16),
        w_mid_v=((27, 64, 64), BF16),
        w_down_v=((8, 32, 64), BF16),
        w_up_v=((8, 32, 64), BF16),
        w_in_v=((27, 32), BF16),
        head_v=((3, 32), BF16),
        meta=((nx, 16, 128), BF16),
        xgi=((nx, 32, 128), BF16),
        xgt=((nx, 96, 128), BF16),
        pli=((ny, 16, 128), BF16),
        plt=((ny, 48, 128), BF16),
        yri=((ny, 16, 128), BF16),
        yrt=((ny, 48, 128), BF16),
        mi=((16, 128), BF16),
        mt=((48, 128), BF16),
        hri=((5, 3, 16, 128), BF16),
        hrt=((3, 3, 48, 128), BF16),
        w0=((256, 32), BF16),
        w1=((256, 1024), BF16),
        w1b=((256, 1024), BF16),
        wm=((64, 768), BF16),
        wmb=((64, 768), BF16),
        tcol=((176, wide), BF16),
        tgt=((6, 32, wide), F32),
        h0s=((10, 256, wide), BF16),
        c0=((20, 256, wide), BF16),
        h1s=((8, 256, wide), BF16),
        cd=((8, 256, wide), BF16),
        qs=((6, 64, wide), BF16),
        ss=((6, 256, wide), BF16),
        gls=((6, 32, wide), BF16),
        gss=((6, 256, wide), BF16),
        cg=((6, 256, wide), BF16),
        gds=((4, 64, wide), BF16),
        cr=((8, 256, wide), BF16),
        grs=((4, 256, wide), BF16),
        gas=((2, 256, 128), BF16),
        errs=((6, 32, wide), BF16),
        vec=((ROWS, 128), F32),
        err=((48, 128), BF16),
        rc=((half, 128), F32),
        ac=((half, 128), F32),
        rx=((nx, rows_x, 128), F32),
        ax=((rows_x, 128), F32),
        ry=((ny, rows_y, 128), F32),
        ay=((rows_y, 128), F32),
        rz=((nzc, rows_y, 128), F32),
        gy=((ny, rows_y, 128), F32),
        gx=((nx, rows_x, 128), F32),
        gc=((nx, rows_x, 128), F32),
        ey=((ny, 48, 128), BF16),
        em=((nx, 96, 128), BF16),
        ex=((nx, 96, 128), BF16),
    )
    sems = dict(loaded=10)
    for kind, count in (
        ("name", nx),
        ("ix", nx),
        ("tx", nx),
        ("iy", ny),
        ("ty", ny),
        ("in", 14),
        ("tn", 14),
        ("ey", ny),
        ("ex", nx),
        ("c", 2),
        ("x", nx),
        ("y", ny),
        ("z", nzc),
        ("gy", ny),
        ("gx", nx),
    ):
        sems["s_" + kind] = count
        sems["r_" + kind] = count
    names = list(operands) + ["out", "tiles"] + list(buffers) + list(sems)
    return pl.pallas_call(
        functools.partial(whole_kernel, nx, ny, ng, names),
        out_shape=(
            jax.ShapeDtypeStruct((ROWS, 128), F32),
            jax.ShapeDtypeStruct((96, 128), BF16),
        ),
        in_specs=[pl.BlockSpec(memory_space=pltpu.MemorySpace.HBM)] * len(operands),
        out_specs=(VM, VM),
        scratch_shapes=[pltpu.VMEM(shape, dtype) for shape, dtype in buffers.values()]
        + [pltpu.SemaphoreType.DMA((count,)) for count in sems.values()],
        compiler_params=pltpu.CompilerParams(
            collective_id=0, has_side_effects=True, vmem_limit_bytes=40 << 20
        ),
        name="whole",
    )(*operands.values())


def unpack_kernel(vec, tiles, err, g_in, g_res, g_down, g_mid, g_up, g_head, lines):
    err[...] = tiles[...]
    for zy in range(9):
        strip = vec[RES + zy * 32 : RES + zy * 32 + 32, :]
        for c in range(3):
            part = strip if c == 0 else pltpu.roll(strip, 128 - 32 * c, 1)
            g_res[zy * 3 + c] = part[:, 0:32]
    for t in range(27):
        a, b, c = t // 9, t // 3 % 3, t % 3
        if b == 1:
            at = MID + (a * 2 + c // 2) * 64
            part = vec[at : at + 64, :]
            if c % 2:
                part = pltpu.roll(part, 64, 1)
            g_mid[t] = part[:, 0:64]
        else:
            g_mid[t] = jnp.zeros((64, 64), F32)
    for pos in range(8):
        quarter = pos & 3
        for at, grad in ((DOWN, g_down), (UP, g_up)):
            part = vec[at + quarter * 32 : at + quarter * 32 + 32, :]
            if pos >> 2:
                part = pltpu.roll(part, 64, 1)
            grad[tap_of(pos)] = part[:, 0:64]
        part = vec[INP + (pos >> 2) * 32 : INP + (pos >> 2) * 32 + 32, :]
        if quarter:
            part = pltpu.roll(part, 128 - 32 * quarter, 1)
        lines[pos] = part
    for t in range(27):
        dz, dy, dx = t // 9, t // 3 % 3, t % 3
        total = None
        for pos in range(8):
            xo, zo, yo = pos >> 2, pos >> 1 & 1, pos & 1
            if 0 <= yo + dy - 1 < 2:
                at = (zo + dz) * 8 + (xo + dx) * 2 + yo + dy - 1
                line = lines[pos, at : at + 1, :]
                total = line if total is None else total + line
        g_in[t : t + 1, :] = total[:, 0:32]
    g_head[...] = vec[HEAD : HEAD + 8, :][0:3, 0:32]


def unpack(vec, tiles):
    return pl.pallas_call(
        unpack_kernel,
        out_shape=(
            jax.ShapeDtypeStruct((96, 128), BF16),
            jax.ShapeDtypeStruct((27, 32), F32),
            jax.ShapeDtypeStruct((27, 32, 32), F32),
            jax.ShapeDtypeStruct((8, 32, 64), F32),
            jax.ShapeDtypeStruct((27, 64, 64), F32),
            jax.ShapeDtypeStruct((8, 32, 64), F32),
            jax.ShapeDtypeStruct((3, 32), F32),
        ),
        in_specs=[VM] * 2,
        out_specs=(VM,) * 7,
        scratch_shapes=[pltpu.VMEM((8, 32, 128), F32)],
        compiler_params=pltpu.CompilerParams(vmem_limit_bytes=32 << 20),
        name="unpack",
    )(vec, tiles)


def local(
    tile_image, tile_target, owner_counts, tile_list, w_in, w_res, w_down, w_mid, w_up, head_weight
):
    ranks = lax.axis_size("xy")
    ng = lax.axis_size("gz")
    nx, ny = grid_of(ranks)
    operands = dict(
        img=tile_image.reshape(SLOTS * 8, 128),
        target=tile_target.reshape(SLOTS * 24, 128),
        counts=owner_counts,
        tile_list=tile_list.reshape(1, SLOTS),
        w_in=w_in,
        w_res=w_res.reshape(9, 3, 32, 32),
        w_down=jnp.transpose(w_down, (0, 2, 1)),
        w_mid=w_mid,
        w_up=w_up,
        head=head_weight,
    )
    sums, tiles = whole(nx, ny, ng, operands)
    tiles, g_in, g_res, g_down, g_mid, g_up, g_head = unpack(sums, tiles)
    tiles = tiles.reshape(1, 1, SLOTS, 3, 4, 2, 128)
    return (tiles, g_in, g_res, jnp.transpose(g_down, (0, 2, 1)), g_mid, g_up, g_head)


def solution(mesh):
    return jax.shard_map(
        local,
        mesh=mesh,
        in_specs=(
            P("gz", "xy", None, None, None, None),
            P("gz", "xy", None, None, None, None, None),
            P("gz", "xy"),
            P("gz", "xy", None),
            P(),
            P(),
            P(),
            P(),
            P(),
            P(),
        ),
        out_specs=(P("gz", "xy", None, None, None, None, None), P(), P(), P(), P(), P(), P()),
        check_vma=False,
    )
```

time: 603 us -> 80.9 us (0.13)
  blocking collectives: 226 us -> 0 us
  waiting for transfers between devices: 183 us -> 0 us
  starting transfers between devices: 96.5 us -> 0 us
  Pallas kernels: 0 us -> 73.4 us
  matrix products: 39.2 us -> 0 us
  local copies, waits for them, and re-layouts: 30.5 us -> 5.73 us
  between operations: 16.6 us -> 1.33 us
  other arithmetic: 7.79 us -> 0 us
    psum x1 -> x0, waiting for transfers between devices: 155 us -> none  [local(): lax.psum((grad_in, grad_res, grad_down, grad_mid, grad_up, head_weight_gr...]
    psum x1 -> x0, blocking collectives: 111 us -> none  [local(): lax.psum((grad_in, grad_res, grad_down, grad_mid, grad_up, head_weight_gr...]
    all_gather x3 -> x0, blocking collectives: 97.2 us -> none  [the longest x1 36.3 us: local(): piece_tgt = lax.all_gather(tile_target, 'xy', axis=1, tiled=True)]
    ppermute x20 -> x0, starting transfers between devices: 87.1 us -> none  [the longest x10 70.6 us: with_halo(): lax.ppermute(tail, axis, [(i, (i + 1) % count) for i in range(ends)])]
    pallas_call x0 -> x2, Pallas kernels: none -> 73.4 us  [the longest x1 72 us: whole(): pl.pallas_call(functools.partial(whole_kernel, nx, ny, ng, names), out_sh...]
    dot_general x227 -> x0, matrix products: 39.2 us -> none  [the longest x108 20.8 us: convolve(): jnp.einsum('oc,czyx->ozyx', weights[tap], window, preferred_element_type=...]
    ppermute x20 -> x0, waiting for transfers between devices: 28.4 us -> none  [the longest x10 28.3 us: with_halo(): lax.ppermute(head, axis, [((i + 1) % count, i) for i in range(ends)])]
    unnamed x1 -> x0, blocking collectives: 18 us -> none
  transfers between devices with their start and end apart: 22 -> 0, of which waited for: 10 -> 0; matrix products, arithmetic and copies ran while one was open for 6% -> 0% of each run, Pallas kernels for 0% -> 0%
where the time goes in v3:
time: 80.9 us; the launch traced here: 80.5 us
  Pallas kernels  73.4 us (91%)
  local copies, waits for them, and re-layouts  5.73 us (7%)
  between operations  1.33 us (2%)
    pallas_call x1, Pallas kernels, whole(): pl.pallas_call(functools.partial(whole_kernel, nx, ny, ng, names), out_sh...  72 us
    unnamed x18, local copies, waits for them, and re-layouts  5.73 us

profile of v3, /device:TPU:1, one launch (start us, length us, event | category | flops | bytes accessed | tf_op | source)
XLA Modules:
  0.0 80.5 jit_solution(6333804066402169607)
XLA Ops:
  0.6 0.0 copy-start.5
  1.3 0.0 copy-start.7
  1.3 0.0 copy-start.8
  1.3 0.0 copy-done.5
  1.3 0.7 copy-done.7
  2.0 0.0 copy-done.8
  2.0 0.0 copy-start
  2.0 1.0 %copy-done = bf16[27,64,64]{2,1,0:T(8,128)(2,1)S(1)} copy-done((bf16[27,64,64]{2,1,0:T(8,128)(2,1)S(1)}, bf16[27,64,64]{2,1,0:T(8,128)(2,1)}, u32[]{:S(2)}) %copy-start) | copy-done | bytes 221208
  3.0 0.0 copy-start.1
  3.0 0.9 %copy-done.1 = bf16[27,32,32]{2,1,0:T(8,128)(2,1)S(1)} copy-done((bf16[27,32,32]{2,1,0:T(8,128)(2,1)S(1)}, bf16[27,32,32]{2,1,0:T(8,128)(2,1)}, u32[]{:S(2)}) %copy-start.1) | copy-done | bytes 55320
  3.9 0.0 copy-start.2
  3.9 0.8 %copy-done.2 = bf16[8,64,32]{1,2,0:T(8,128)(2,1)S(1)} copy-done((bf16[8,64,32]{1,2,0:T(8,128)(2,1)S(1)}, bf16[8,64,32]{1,2,0:T(8,128)(2,1)}, u32[]{:S(2)}) %copy-start.2) | copy-done | bytes 32792
  4.8 0.0 copy-start.3
  4.8 0.8 %copy-done.3 = bf16[8,32,64]{2,1,0:T(8,128)(2,1)S(1)} copy-done((bf16[8,32,64]{2,1,0:T(8,128)(2,1)S(1)}, bf16[8,32,64]{2,1,0:T(8,128)(2,1)}, u32[]{:S(2)}) %copy-start.3) | copy-done | bytes 32792
  5.6 0.0 copy-start.4
  5.6 0.7 copy-done.4
  6.4 0.0 copy-start.6
  6.4 0.7 copy-done.6
  7.1 72.0 %whole.1 = (f32[1024,128]{1,0:T(8,128)S(1)}, bf16[96,128]{1,0:T(8,128)(2,1)S(1)}) custom-call(bf16[32,128]{1,0:T(8,128)(2,1)S(1)} %bitcast.10, bf16[96,128]{1,0:T(8,128)(2,1)S(1)} %bitcast.9, s32[1,1]{1,0:T(1,128)S(6)} %copy.17.refs_2_, s32[1,4]{1,0:T(1,128)S(1)} %bitcast.11, bf16[27,32]{1,0:T(8,128)(2,1)S(1)} %copy-done.6, ...), custom_call_target="tpu_custom_call" | custom-call | tf_op jit(solution)/shard_map/whole/pallas_call | solution.py:639
  79.1 1.4 %unpack.1 = (bf16[96,128]{1,0:T(8,128)(2,1)}, f32[27,32]{1,0:T(8,128)}, f32[27,32,32]{2,1,0:T(8,128)}, f32[8,32,64]{2,1,0:T(8,128)}, f32[27,64,64]{2,1,0:T(8,128...) custom-call(f32[1024,128]{1,0:T(8,128)S(1)} %get-tuple-element.16.vec, bf16[96,128]{1,0:T(8,128)(2,1)S(1)} %get-tuple-element.17.tiles), custom_call_target="tpu_custom_call" | custom-call | tf_op jit(solution)/shard_map/unpack/pallas_call | solution.py:698
Async XLA Ops:
  0.6 0.7 copy-start.5
  1.3 0.7 copy-start.7
  1.3 0.7 copy-start.8
  2.0 1.0 %copy-start = (bf16[27,64,64]{2,1,0:T(8,128)(2,1)S(1)}, bf16[27,64,64]{2,1,0:T(8,128)(2,1)}, u32[]{:S(2)}) copy-start(bf16[27,64,64]{2,1,0:T(8,128)(2,1)} %refs_7_.1) | copy-start | bytes 663556
  3.0 0.9 %copy-start.1 = (bf16[27,32,32]{2,1,0:T(8,128)(2,1)S(1)}, bf16[27,32,32]{2,1,0:T(8,128)(2,1)}, u32[]{:S(2)}) copy-start(bf16[27,32,32]{2,1,0:T(8,128)(2,1)} %param.15) | copy-start | bytes 165892
  3.9 0.8 %copy-start.2 = (bf16[8,64,32]{1,2,0:T(8,128)(2,1)S(1)}, bf16[8,64,32]{1,2,0:T(8,128)(2,1)}, u32[]{:S(2)}) copy-start(bf16[8,64,32]{1,2,0:T(8,128)(2,1)} %param.16) | copy-start | bytes 98308
  4.8 0.8 %copy-start.3 = (bf16[8,32,64]{2,1,0:T(8,128)(2,1)S(1)}, bf16[8,32,64]{2,1,0:T(8,128)(2,1)}, u32[]{:S(2)}) copy-start(bf16[8,32,64]{2,1,0:T(8,128)(2,1)} %refs_8_.1) | copy-start | bytes 98308
  5.6 0.7 copy-start.4
  6.4 0.7 copy-start.6

commit v4 on v3

--- a/solution.py
+++ b/solution.py
@@ -450,7 +450,6 @@
 
     half = ROWS // CORES
     rows_x = half // nx
-    rows_y = rows_x // ny
 
     def piece(k, size):
         return pl.ds(pl.multiple_of(k * size, size), size)
@@ -492,40 +491,42 @@
     total = r.ac[piece(xi, rows_x), :]
     for k in range(1, nx):
         total = total + r.rx[k]
-    r.ax[...] = total
-    over_y = [
-        remote(r.ax.at[piece(y_at[k], rows_y)], r.ry.at[k], r.s_y.at[k], r.r_y.at[k], y_peer[k])
-        for k in range(1, ny)
-    ]
-    for copy in over_y:
-        copy.start()
-    for copy in over_y:
-        copy.wait_recv()
-    total = r.ax[piece(yi, rows_y), :]
-    for k in range(1, ny):
-        total = total + r.ry[k]
-    r.ay[...] = total
-    over_z = [remote(r.ay, r.rz.at[zi], r.s_z.at[k], r.r_z.at[k], z_peer[k]) for k in range(1, nzc)]
-    for copy in over_z:
-        copy.start()
-    r.rz[zi] = r.ay[...]
-    for k in range(1, nzc):
-        at = lax.rem(zi - k + nzc, nzc)
-        remote(r.ay, r.rz.at[at], r.s_z.at[k], r.r_z.at[k], z_peer[k]).wait_recv()
-    total = r.rz[0]
-    for k in range(1, nzc):
-        total = total + r.rz[k]
-    r.gy[yi] = total
-    back_y = [
-        remote(r.gy.at[yi], r.gy.at[yi], r.s_gy.at[k], r.r_gy.at[k], y_peer[k])
-        for k in range(1, ny)
-    ]
-    for copy in back_y:
-        copy.start()
-    for k in range(1, ny):
-        at = lax.rem(yi - k + ny, ny)
-        remote(r.gy.at[at], r.gy.at[at], r.s_gy.at[k], r.r_gy.at[k], y_peer[k]).wait_recv()
-    r.gx[xi] = r.gy[...].reshape(rows_x, 128)
+
+    def share(buf, at, peers, send, recv):
+        return [
+            remote(buf.at[at], buf.at[at], send.at[k], recv.at[k], peers[k])
+            for k in range(1, len(peers))
+        ]
+
+    def gathered(buf, at, peers, send, recv):
+        count = len(peers)
+        for k in range(1, count):
+            where = lax.rem(at - k + count, count)
+            remote(buf.at[where], buf.at[where], send.at[k], recv.at[k], peers[k]).wait_recv()
+        total = buf[0].astype(F32)
+        for n in range(1, count):
+            total = total + buf[n].astype(F32)
+        return total
+
+    part = rows_x // 2
+    r.ya[yi] = total[0:part].astype(r.ya.dtype)
+    y_first = share(r.ya, yi, y_peer, r.s_ya, r.r_ya)
+    for copy in y_first:
+        copy.start()
+    r.za[zi] = total[part:].astype(r.za.dtype)
+    z_first = share(r.za, zi, z_peer, r.s_za, r.r_za)
+    for copy in z_first:
+        copy.start()
+    r.zb[zi] = gathered(r.ya, yi, y_peer, r.s_ya, r.r_ya).astype(r.zb.dtype)
+    z_then = share(r.zb, zi, z_peer, r.s_zb, r.r_zb)
+    for copy in z_then:
+        copy.start()
+    r.yb[yi] = gathered(r.za, zi, z_peer, r.s_za, r.r_za).astype(r.yb.dtype)
+    y_then = share(r.yb, yi, y_peer, r.s_yb, r.r_yb)
+    for copy in y_then:
+        copy.start()
+    r.gx[xi, 0:part] = gathered(r.zb, zi, z_peer, r.s_zb, r.r_zb)
+    r.gx[xi, part:] = gathered(r.yb, yi, y_peer, r.s_yb, r.r_yb)
     back_x = [
         remote(r.gx.at[xi], r.gx.at[xi], r.s_gx.at[k], r.r_gx.at[k], x_peer[k])
         for k in range(1, nx)
@@ -548,7 +549,7 @@
     r.out[piece(1 - core, half), :] = r.gc[...].reshape(half, 128)
     sent = [swap, back_c] + name_x + img_x + tgt_x + img_n + tgt_n + err_y + err_x
     sent += [img_y(k) for k in range(1, ny)] + [tgt_y(k) for k in range(1, ny)]
-    for copy in sent + over_x + over_y + over_z + back_y + back_x:
+    for copy in sent + over_x + y_first + z_first + z_then + y_then + back_x:
         copy.wait_send()
 
 
@@ -557,7 +558,6 @@
     nzc = ng // CORES
     half = ROWS // CORES
     rows_x = half // nx
-    rows_y = rows_x // ny
     buffers = dict(
         list_v=((1, SLOTS), jnp.int32),
         count_v=((1, 1), jnp.int32),
@@ -604,11 +604,10 @@
         rc=((half, 128), F32),
         ac=((half, 128), F32),
         rx=((nx, rows_x, 128), F32),
-        ax=((rows_x, 128), F32),
-        ry=((ny, rows_y, 128), F32),
-        ay=((rows_y, 128), F32),
-        rz=((nzc, rows_y, 128), F32),
-        gy=((ny, rows_y, 128), F32),
+        ya=((ny, rows_x // 2, 128), F32),
+        za=((nzc, rows_x // 2, 128), F32),
+        yb=((ny, rows_x // 2, 128), F32),
+        zb=((nzc, rows_x // 2, 128), F32),
         gx=((nx, rows_x, 128), F32),
         gc=((nx, rows_x, 128), F32),
         ey=((ny, 48, 128), BF16),
@@ -628,9 +627,10 @@
         ("ex", nx),
         ("c", 2),
         ("x", nx),
-        ("y", ny),
-        ("z", nzc),
-        ("gy", ny),
+        ("ya", ny),
+        ("za", nzc),
+        ("yb", ny),
+        ("zb", nzc),
         ("gx", nx),
     ):
         sems["s_" + kind] = count
@@ -647,14 +647,23 @@
         scratch_shapes=[pltpu.VMEM(shape, dtype) for shape, dtype in buffers.values()]
         + [pltpu.SemaphoreType.DMA((count,)) for count in sems.values()],
         compiler_params=pltpu.CompilerParams(
-            collective_id=0, has_side_effects=True, vmem_limit_bytes=40 << 20
+            collective_id=0, has_side_effects=True, vmem_limit_bytes=56 << 20
         ),
         name="whole",
     )(*operands.values())
 
 
-def unpack_kernel(vec, tiles, err, g_in, g_res, g_down, g_mid, g_up, g_head, lines):
-    err[...] = tiles[...]
+def unpack_kernel(
+    sums, tiles, err, g_in, g_res, g_down, g_mid, g_up, g_head, lines, vec, sems
+):
+    load = pltpu.make_async_copy(sums, vec, sems.at[0])
+    load.start()
+    load_err = pltpu.make_async_copy(tiles, err, sems.at[1])
+    load_err.start()
+    for t in range(27):
+        if t // 3 % 3 != 1:
+            g_mid[t] = jnp.zeros((64, 64), F32)
+    load.wait()
     for zy in range(9):
         strip = vec[RES + zy * 32 : RES + zy * 32 + 32, :]
         for c in range(3):
@@ -668,8 +677,6 @@
             if c % 2:
                 part = pltpu.roll(part, 64, 1)
             g_mid[t] = part[:, 0:64]
-        else:
-            g_mid[t] = jnp.zeros((64, 64), F32)
     for pos in range(8):
         quarter = pos & 3
         for at, grad in ((DOWN, g_down), (UP, g_up)):
@@ -692,6 +699,7 @@
                 total = line if total is None else total + line
         g_in[t : t + 1, :] = total[:, 0:32]
     g_head[...] = vec[HEAD : HEAD + 8, :][0:3, 0:32]
+    load_err.wait()
 
 
 def unpack(vec, tiles):
@@ -706,10 +714,14 @@
             jax.ShapeDtypeStruct((8, 32, 64), F32),
             jax.ShapeDtypeStruct((3, 32), F32),
         ),
-        in_specs=[VM] * 2,
+        in_specs=[pl.BlockSpec(memory_space=pltpu.MemorySpace.HBM)] * 2,
         out_specs=(VM,) * 7,
-        scratch_shapes=[pltpu.VMEM((8, 32, 128), F32)],
-        compiler_params=pltpu.CompilerParams(vmem_limit_bytes=32 << 20),
+        scratch_shapes=[
+            pltpu.VMEM((8, 32, 128), F32),
+            pltpu.VMEM((ROWS, 128), F32),
+            pltpu.SemaphoreType.DMA((2,)),
+        ],
+        compiler_params=pltpu.CompilerParams(vmem_limit_bytes=56 << 20),
         name="unpack",
     )(vec, tiles)
 

time: 80.9 us -> 76.5 us (0.946)
  local copies, waits for them, and re-layouts: 5.73 us -> 0 us
  Pallas kernels: 73.4 us -> 75 us
    unnamed x18 -> x0, local copies, waits for them, and re-layouts: 5.73 us -> none
    pallas_call x1, Pallas kernels: 1.38 us -> 2.48 us  [unpack(): pl.pallas_call(unpack_kernel, out_shape=(jax.ShapeDtypeStruct((96, 128),...]
where the time goes in v4:
time: 76.5 us; the launch traced here: 76.3 us
  Pallas kernels  75 us (98%)
  between operations  1.29 us (2%)
    pallas_call x1, Pallas kernels, whole(): pl.pallas_call(functools.partial(whole_kernel, nx, ny, ng, names), out_sh...  72.5 us
    pallas_call x1, Pallas kernels, unpack(): pl.pallas_call(unpack_kernel, out_shape=(jax.ShapeDtypeStruct((96, 128),...  2.48 us

profile of v4, /device:TPU:1, one launch (start us, length us, event | category | flops | bytes accessed | tf_op | source)
XLA Modules:
  0.0 76.3 jit_solution(3605717073452817252)
XLA Ops:
  1.3 72.5 %whole.1 = (f32[1024,128]{1,0:T(8,128)}, bf16[96,128]{1,0:T(8,128)(2,1)}) custom-call(bf16[32,128]{1,0:T(8,128)(2,1)} %bitcast.10, bf16[96,128]{1,0:T(8,128)(2,1)} %bitcast.9, s32[1,1]{1,0:T(1,128)S(6)} %copy.17.refs_2_, s32[1,4]{1,0:T(1,128)} %bitcast.11, bf16[27,32]{1,0:T(8,128)(2,1)} %refs_4_.1, bf16[9,3,32,32]{3,2,1,0:T(8,128)(2,1)} %bitcast.7, ...), custom_call_target="tpu_custom_call" | custom-call | tf_op jit(solution)/shard_map/whole/pallas_call | solution.py:639
  73.8 2.5 %unpack.1 = (bf16[96,128]{1,0:T(8,128)(2,1)}, f32[27,32]{1,0:T(8,128)}, f32[27,32,32]{2,1,0:T(8,128)}, f32[8,32,64]{2,1,0:T(8,128)}, f32[27,64,64]{2,1,0:T(8,128...) custom-call(f32[1024,128]{1,0:T(8,128)} %get-tuple-element.16.sums, bf16[96,128]{1,0:T(8,128)(2,1)} %get-tuple-element.17.tiles), custom_call_target="tpu_custom_call" | custom-call | tf_op jit(solution)/shard_map/unpack/pallas_call | solution.py:706

commit v5 on v4

--- a/solution.py
+++ b/solution.py
@@ -484,7 +484,7 @@
         remote(r.em.at[nx - k], r.ex.at[k], r.s_ex.at[k], r.r_ex.at[k], x_peer[k])
         for k in range(1, nx)
     ]
-    for copy in over_x + err_x:
+    for copy in over_x:
         copy.start()
     for copy in over_x:
         copy.wait_recv()
@@ -515,7 +515,7 @@
         copy.start()
     r.za[zi] = total[part:].astype(r.za.dtype)
     z_first = share(r.za, zi, z_peer, r.s_za, r.r_za)
-    for copy in z_first:
+    for copy in z_first + err_x:
         copy.start()
     r.zb[zi] = gathered(r.ya, yi, y_peer, r.s_ya, r.r_ya).astype(r.zb.dtype)
     z_then = share(r.zb, zi, z_peer, r.s_zb, r.r_zb)
@@ -538,7 +538,16 @@
         remote(r.gx.at[at], r.gx.at[at], r.s_gx.at[k], r.r_gx.at[k], x_peer[k]).wait_recv()
     back_c = remote(r.gx, r.gc, r.s_c.at[1], r.r_c.at[1], other)
     back_c.start()
-    r.out[piece(core, half), :] = r.gx[...].reshape(half, 128)
+    def store(buf, side, at):
+        rows = lambda n: pl.ds(pl.multiple_of(side * half + n * rows_x, rows_x), rows_x)
+        return [
+            pltpu.make_async_copy(buf.at[n], r.out.at[rows(n)], r.stored.at[at, n])
+            for n in range(nx)
+        ]
+
+    stores = store(r.gx, core, 0)
+    for copy in stores:
+        copy.start()
     for copy in err_x:
         copy.wait_recv()
     total = r.em[0].astype(F32)
@@ -546,7 +555,11 @@
         total = total + r.ex[k].astype(F32)
     r.tiles[...] = total.astype(BF16)
     back_c.wait_recv()
-    r.out[piece(1 - core, half), :] = r.gc[...].reshape(half, 128)
+    last = store(r.gc, 1 - core, 1)
+    for copy in last:
+        copy.start()
+    for copy in stores + last:
+        copy.wait()
     sent = [swap, back_c] + name_x + img_x + tgt_x + img_n + tgt_n + err_y + err_x
     sent += [img_y(k) for k in range(1, ny)] + [tgt_y(k) for k in range(1, ny)]
     for copy in sent + over_x + y_first + z_first + z_then + y_then + back_x:
@@ -604,10 +617,10 @@
         rc=((half, 128), F32),
         ac=((half, 128), F32),
         rx=((nx, rows_x, 128), F32),
-        ya=((ny, rows_x // 2, 128), F32),
-        za=((nzc, rows_x // 2, 128), F32),
-        yb=((ny, rows_x // 2, 128), F32),
-        zb=((nzc, rows_x // 2, 128), F32),
+        ya=((ny, rows_x // 2, 128), BF16),
+        za=((nzc, rows_x // 2, 128), BF16),
+        yb=((ny, rows_x // 2, 128), BF16),
+        zb=((nzc, rows_x // 2, 128), BF16),
         gx=((nx, rows_x, 128), F32),
         gc=((nx, rows_x, 128), F32),
         ey=((ny, 48, 128), BF16),
@@ -635,7 +648,7 @@
     ):
         sems["s_" + kind] = count
         sems["r_" + kind] = count
-    names = list(operands) + ["out", "tiles"] + list(buffers) + list(sems)
+    names = list(operands) + ["out", "tiles"] + list(buffers) + list(sems) + ["stored"]
     return pl.pallas_call(
         functools.partial(whole_kernel, nx, ny, ng, names),
         out_shape=(
@@ -643,9 +656,10 @@
             jax.ShapeDtypeStruct((96, 128), BF16),
         ),
         in_specs=[pl.BlockSpec(memory_space=pltpu.MemorySpace.HBM)] * len(operands),
-        out_specs=(VM, VM),
+        out_specs=(pl.BlockSpec(memory_space=pltpu.MemorySpace.HBM), VM),
         scratch_shapes=[pltpu.VMEM(shape, dtype) for shape, dtype in buffers.values()]
-        + [pltpu.SemaphoreType.DMA((count,)) for count in sems.values()],
+        + [pltpu.SemaphoreType.DMA((count,)) for count in sems.values()]
+        + [pltpu.SemaphoreType.DMA((2, nx))],
         compiler_params=pltpu.CompilerParams(
             collective_id=0, has_side_effects=True, vmem_limit_bytes=56 << 20
         ),
@@ -656,19 +670,24 @@
 def unpack_kernel(
     sums, tiles, err, g_in, g_res, g_down, g_mid, g_up, g_head, lines, vec, sems
 ):
-    load = pltpu.make_async_copy(sums, vec, sems.at[0])
-    load.start()
-    load_err = pltpu.make_async_copy(tiles, err, sems.at[1])
-    load_err.start()
+    ends = (RES, MID, DOWN, INP, USED)
+    loads = [
+        pltpu.make_async_copy(sums.at[a:b], vec.at[a:b], sems.at[n])
+        for n, (a, b) in enumerate(zip(ends[:-1], ends[1:]))
+    ]
+    load_err = pltpu.make_async_copy(tiles, err, sems.at[4])
+    for copy in loads + [load_err]:
+        copy.start()
     for t in range(27):
         if t // 3 % 3 != 1:
             g_mid[t] = jnp.zeros((64, 64), F32)
-    load.wait()
+    loads[0].wait()
     for zy in range(9):
         strip = vec[RES + zy * 32 : RES + zy * 32 + 32, :]
         for c in range(3):
             part = strip if c == 0 else pltpu.roll(strip, 128 - 32 * c, 1)
             g_res[zy * 3 + c] = part[:, 0:32]
+    loads[1].wait()
     for t in range(27):
         a, b, c = t // 9, t // 3 % 3, t % 3
         if b == 1:
@@ -677,6 +696,8 @@
             if c % 2:
                 part = pltpu.roll(part, 64, 1)
             g_mid[t] = part[:, 0:64]
+    loads[2].wait()
+    loads[3].wait()
     for pos in range(8):
         quarter = pos & 3
         for at, grad in ((DOWN, g_down), (UP, g_up)):
@@ -719,7 +740,7 @@
         scratch_shapes=[
             pltpu.VMEM((8, 32, 128), F32),
             pltpu.VMEM((ROWS, 128), F32),
-            pltpu.SemaphoreType.DMA((2,)),
+            pltpu.SemaphoreType.DMA((5,)),
         ],
         compiler_params=pltpu.CompilerParams(vmem_limit_bytes=56 << 20),
         name="unpack",

time: 76.5 us -> 73.7 us (0.963)
  Pallas kernels: 75 us -> 72.3 us
    pallas_call x1, Pallas kernels: 72.5 us -> 69.8 us  [whole(): pl.pallas_call(functools.partial(whole_kernel, nx, ny, ng, names), out_sh...]
where the time goes in v5:
time: 73.7 us; the launch traced here: 73.6 us
  Pallas kernels  72.3 us (98%)
  between operations  1.29 us (2%)
    pallas_call x1, Pallas kernels, whole(): pl.pallas_call(functools.partial(whole_kernel, nx, ny, ng, names), out_sh...  69.8 us
    pallas_call x1, Pallas kernels, unpack(): pl.pallas_call(unpack_kernel, out_shape=(jax.ShapeDtypeStruct((96, 128),...  2.5 us

profile of v5, /device:TPU:1, one launch (start us, length us, event | category | flops | bytes accessed | tf_op | source)
XLA Modules:
  0.0 73.6 jit_solution(11905786128222044792)
XLA Ops:
  1.3 69.8 %whole.1 = (f32[1024,128]{1,0:T(8,128)}, bf16[96,128]{1,0:T(8,128)(2,1)}) custom-call(bf16[32,128]{1,0:T(8,128)(2,1)} %bitcast.10, bf16[96,128]{1,0:T(8,128)(2,1)} %bitcast.9, s32[1,1]{1,0:T(1,128)S(6)} %copy.17.refs_2_, s32[1,4]{1,0:T(1,128)} %bitcast.11, bf16[27,32]{1,0:T(8,128)(2,1)} %refs_4_.1, bf16[9,3,32,32]{3,2,1,0:T(8,128)(2,1)} %bitcast.7, ...), custom_call_target="tpu_custom_call" | custom-call | tf_op jit(solution)/shard_map/whole/pallas_call | solution.py:652
  71.1 2.5 %unpack.1 = (bf16[96,128]{1,0:T(8,128)(2,1)}, f32[27,32]{1,0:T(8,128)}, f32[27,32,32]{2,1,0:T(8,128)}, f32[8,32,64]{2,1,0:T(8,128)}, f32[27,64,64]{2,1,0:T(8,128...) custom-call(f32[1024,128]{1,0:T(8,128)} %get-tuple-element.16.sums, bf16[96,128]{1,0:T(8,128)(2,1)} %get-tuple-element.17.tiles), custom_call_target="tpu_custom_call" | custom-call | tf_op jit(solution)/shard_map/unpack/pallas_call | solution.py:727

commit v6 on v5

--- a/solution.py
+++ b/solution.py
@@ -476,8 +476,9 @@
     lax.fori_loop(0, nx, answer, 0)
     swap.wait_recv()
     r.ac[...] = r.vec[piece(core, half), :] + r.rc[...]
+    r.ab[...] = r.ac[...].astype(BF16)
     over_x = [
-        remote(r.ac.at[piece(x_at[k], rows_x)], r.rx.at[k], r.s_x.at[k], r.r_x.at[k], x_peer[k])
+        remote(r.ab.at[piece(x_at[k], rows_x)], r.rx.at[k], r.s_x.at[k], r.r_x.at[k], x_peer[k])
         for k in range(1, nx)
     ]
     err_x = [
@@ -490,7 +491,7 @@
         copy.wait_recv()
     total = r.ac[piece(xi, rows_x), :]
     for k in range(1, nx):
-        total = total + r.rx[k]
+        total = total + r.rx[k].astype(F32)
 
     def share(buf, at, peers, send, recv):
         return [
@@ -525,8 +526,8 @@
     y_then = share(r.yb, yi, y_peer, r.s_yb, r.r_yb)
     for copy in y_then:
         copy.start()
-    r.gx[xi, 0:part] = gathered(r.zb, zi, z_peer, r.s_zb, r.r_zb)
-    r.gx[xi, part:] = gathered(r.yb, yi, y_peer, r.s_yb, r.r_yb)
+    r.gx[xi, 0:part] = gathered(r.zb, zi, z_peer, r.s_zb, r.r_zb).astype(BF16)
+    r.gx[xi, part:] = gathered(r.yb, yi, y_peer, r.s_yb, r.r_yb).astype(BF16)
     back_x = [
         remote(r.gx.at[xi], r.gx.at[xi], r.s_gx.at[k], r.r_gx.at[k], x_peer[k])
         for k in range(1, nx)
@@ -616,13 +617,14 @@
         err=((48, 128), BF16),
         rc=((half, 128), F32),
         ac=((half, 128), F32),
-        rx=((nx, rows_x, 128), F32),
+        rx=((nx, rows_x, 128), BF16),
+        ab=((half, 128), BF16),
         ya=((ny, rows_x // 2, 128), BF16),
         za=((nzc, rows_x // 2, 128), BF16),
         yb=((ny, rows_x // 2, 128), BF16),
         zb=((nzc, rows_x // 2, 128), BF16),
-        gx=((nx, rows_x, 128), F32),
-        gc=((nx, rows_x, 128), F32),
+        gx=((nx, rows_x, 128), BF16),
+        gc=((nx, rows_x, 128), BF16),
         ey=((ny, 48, 128), BF16),
         em=((nx, 96, 128), BF16),
         ex=((nx, 96, 128), BF16),
@@ -652,7 +654,7 @@
     return pl.pallas_call(
         functools.partial(whole_kernel, nx, ny, ng, names),
         out_shape=(
-            jax.ShapeDtypeStruct((ROWS, 128), F32),
+            jax.ShapeDtypeStruct((ROWS, 128), BF16),
             jax.ShapeDtypeStruct((96, 128), BF16),
         ),
         in_specs=[pl.BlockSpec(memory_space=pltpu.MemorySpace.HBM)] * len(operands),
@@ -670,7 +672,7 @@
 def unpack_kernel(
     sums, tiles, err, g_in, g_res, g_down, g_mid, g_up, g_head, lines, vec, sems
 ):
-    ends = (RES, MID, DOWN, INP, USED)
+    ends = (RES, MID, DOWN, INP, USED + 8)
     loads = [
         pltpu.make_async_copy(sums.at[a:b], vec.at[a:b], sems.at[n])
         for n, (a, b) in enumerate(zip(ends[:-1], ends[1:]))
@@ -683,7 +685,7 @@
             g_mid[t] = jnp.zeros((64, 64), F32)
     loads[0].wait()
     for zy in range(9):
-        strip = vec[RES + zy * 32 : RES + zy * 32 + 32, :]
+        strip = vec[RES + zy * 32 : RES + zy * 32 + 32, :].astype(F32)
         for c in range(3):
             part = strip if c == 0 else pltpu.roll(strip, 128 - 32 * c, 1)
             g_res[zy * 3 + c] = part[:, 0:32]
@@ -692,7 +694,7 @@
         a, b, c = t // 9, t // 3 % 3, t % 3
         if b == 1:
             at = MID + (a * 2 + c // 2) * 64
-            part = vec[at : at + 64, :]
+            part = vec[at : at + 64, :].astype(F32)
             if c % 2:
                 part = pltpu.roll(part, 64, 1)
             g_mid[t] = part[:, 0:64]
@@ -701,11 +703,11 @@
     for pos in range(8):
         quarter = pos & 3
         for at, grad in ((DOWN, g_down), (UP, g_up)):
-            part = vec[at + quarter * 32 : at + quarter * 32 + 32, :]
+            part = vec[at + quarter * 32 : at + quarter * 32 + 32, :].astype(F32)
             if pos >> 2:
                 part = pltpu.roll(part, 64, 1)
             grad[tap_of(pos)] = part[:, 0:64]
-        part = vec[INP + (pos >> 2) * 32 : INP + (pos >> 2) * 32 + 32, :]
+        part = vec[INP + (pos >> 2) * 32 : INP + (pos >> 2) * 32 + 32, :].astype(F32)
         if quarter:
             part = pltpu.roll(part, 128 - 32 * quarter, 1)
         lines[pos] = part
@@ -719,7 +721,7 @@
                 line = lines[pos, at : at + 1, :]
                 total = line if total is None else total + line
         g_in[t : t + 1, :] = total[:, 0:32]
-    g_head[...] = vec[HEAD : HEAD + 8, :][0:3, 0:32]
+    g_head[...] = vec[HEAD : HEAD + 16, :].astype(F32)[0:3, 0:32]
     load_err.wait()
 
 
@@ -739,7 +741,7 @@
         out_specs=(VM,) * 7,
         scratch_shapes=[
             pltpu.VMEM((8, 32, 128), F32),
-            pltpu.VMEM((ROWS, 128), F32),
+            pltpu.VMEM((ROWS, 128), BF16),
             pltpu.SemaphoreType.DMA((5,)),
         ],
         compiler_params=pltpu.CompilerParams(vmem_limit_bytes=56 << 20),

time: 73.7 us -> 71.9 us (0.976)
  Pallas kernels: 72.3 us -> 70.4 us
    pallas_call x1, Pallas kernels: 69.8 us -> 68 us  [whole(): pl.pallas_call(functools.partial(whole_kernel, nx, ny, ng, names), out_sh...]
where the time goes in v6:
time: 71.9 us; the launch traced here: 71.7 us
  Pallas kernels  70.4 us (98%)
  between operations  1.29 us (2%)
    pallas_call x1, Pallas kernels, whole(): pl.pallas_call(functools.partial(whole_kernel, nx, ny, ng, names), out_sh...  68 us
    pallas_call x1, Pallas kernels, unpack(): pl.pallas_call(unpack_kernel, out_shape=(jax.ShapeDtypeStruct((96, 128),...  2.41 us

profile of v6, /device:TPU:1, one launch (start us, length us, event | category | flops | bytes accessed | tf_op | source)
XLA Modules:
  0.0 71.7 jit_solution(9700832160556836620)
XLA Ops:
  1.3 68.0 %whole.1 = (bf16[1024,128]{1,0:T(8,128)(2,1)}, bf16[96,128]{1,0:T(8,128)(2,1)}) custom-call(bf16[32,128]{1,0:T(8,128)(2,1)} %bitcast.10, bf16[96,128]{1,0:T(8,128)(2,1)} %bitcast.9, s32[1,1]{1,0:T(1,128)S(6)} %copy.17.refs_2_, s32[1,4]{1,0:T(1,128)} %bitcast.11, bf16[27,32]{1,0:T(8,128)(2,1)} %refs_4_.1, bf16[9,3,32,32]{3,2,1,0:T(8,128)(2,1)} %bitcast.7, ...), custom_call_target="tpu_custom_call" | custom-call | tf_op jit(solution)/shard_map/whole/pallas_call | solution.py:654
  69.3 2.4 %unpack.1 = (bf16[96,128]{1,0:T(8,128)(2,1)}, f32[27,32]{1,0:T(8,128)}, f32[27,32,32]{2,1,0:T(8,128)}, f32[8,32,64]{2,1,0:T(8,128)}, f32[27,64,64]{2,1,0:T(8,128...) custom-call(bf16[1024,128]{1,0:T(8,128)(2,1)} %get-tuple-element.16.sums, bf16[96,128]{1,0:T(8,128)(2,1)} %get-tuple-element.17.tiles), custom_call_target="tpu_custom_call" | custom-call | tf_op jit(solution)/shard_map/unpack/pallas_call | solution.py:729
